TPU v7x, 32 devices: a whole 2x2x4 slice. The times are simulated.
32 devices in a mesh: dp: 4 (over y, x), expert: 8 (over z, core).
Axes of the slice: x: 2, y: 2, z: 4, core: 2. Of those that a mesh axis runs over, the one named last changes fastest.
Arguments:
- tokens: bfloat16 [768, 4096], P('expert', 'dp'), may hold values from -6 to 6
- expert_ids: int32 [768, 8], P('expert'), may hold values from 0 to 7, as said below
- gate_probs: float32 [768, 8], P('expert'), may hold values from 0.05 to 1
- gate_weight: bfloat16 [8, 4096, 768], P('expert', 'dp'), may hold values from -0.09375 to 0.09375
- up_weight: bfloat16 [8, 4096, 768], P('expert', 'dp'), may hold values from -0.09375 to 0.09375
- down_weight: bfloat16 [8, 768, 4096], P('expert', None, 'dp'), may hold values from -0.21875 to 0.21875
- out_grad: bfloat16 [768, 4096], P('expert', 'dp'), may hold values from -6 to 6
Outputs:
- layer_out: bfloat16 [768, 4096], P('expert', 'dp')
- token_grad: bfloat16 [768, 4096], P('expert', 'dp')
- gate_grad: bfloat16 [8, 4096, 768], P('expert', 'dp')
- up_grad: bfloat16 [8, 4096, 768], P('expert', 'dp')
- down_grad: bfloat16 [8, 768, 4096], P('expert', None, 'dp')
Inputs may be any that keep to these rules, and one draw needn't show every extreme that they name: `expert_ids`: each row names 8 different experts. Among the 96 rows of one device (aligned blocks) no expert is named by more than 96 rows, and some expert is named by exactly 96 rows in every such block.
All inputs are finite; a program needn't handle non-finite values.
Results may differ from a plain program's by a relative error of at most 0.018.
Values may be sent and summed in bfloat16 or wider, within the bound.
A program may use at most 64 MiB of HBM per device.

v0:
```python
import jax
import jax.numpy as jnp
from jax import lax
from jax.sharding import PartitionSpec as P


def rounded(values):
    return lax.optimization_barrier(values.astype(jnp.bfloat16)).astype(jnp.float32)


def contract_last(first_op, second_op):
    return lax.dot_general(
        first_op, second_op, (((1,), (1,)), ((), ())), preferred_element_type=jnp.float32
    )


def contract_rows(first_op, second_op):
    return lax.dot_general(
        first_op, second_op, (((0,), (0,)), ((), ())), preferred_element_type=jnp.float32
    )


def swish_grads(grad_in, gate_pre, up_pre):
    sigmoid_gate = jax.nn.sigmoid(gate_pre)
    gate_pre_grad = (
        grad_in * up_pre * sigmoid_gate * (1.0 + gate_pre * (1.0 - sigmoid_gate))
    ).astype(jnp.bfloat16)
    up_pre_grad = (grad_in * jax.nn.silu(gate_pre)).astype(jnp.bfloat16)
    return (gate_pre_grad, up_pre_grad)


def send_back(values):
    return lax.all_to_all(values, "expert", split_axis=0, concat_axis=0, tiled=True)


def body(tokens, expert_ids, gate_probs, gate_weight, up_weight, down_weight, out_grad):
    tok_rows, width_part = tokens.shape
    top_count = expert_ids.shape[1]
    groups = lax.axis_size("expert")
    capacity = min(tok_rows, 4 * tok_rows * top_count // (3 * groups))
    slot_count = groups * capacity
    pair_count = tok_rows * top_count
    hidden_units = gate_weight.shape[2]
    w_gate = gate_weight[0]
    w_up = up_weight[0]
    w_down = down_weight[0]
    weights = gate_probs / jnp.sum(gate_probs, axis=1, keepdims=True)
    flat_ids = expert_ids.reshape(pair_count)
    onehot = (flat_ids[:, None] == jnp.arange(groups, dtype=jnp.int32)[None, :]).astype(jnp.int32)
    earlier = jnp.cumsum(onehot, axis=0) - onehot
    position = jnp.sum(earlier * onehot, axis=1)
    slot_of_pair = flat_ids * capacity + position
    pair_of_slot = (
        jnp.full((slot_count,), pair_count, jnp.int32)
        .at[slot_of_pair]
        .set(jnp.arange(pair_count, dtype=jnp.int32))
    )
    token_of_slot = pair_of_slot // top_count
    zero_row = jnp.zeros((1, width_part), jnp.bfloat16)
    send_rows = jnp.concatenate([tokens, zero_row], axis=0)[token_of_slot].reshape(
        groups, capacity, width_part
    )

    def run_blocks(step_fn, initial):
        return step_fn(0, slot_count, initial)

    expert_rows = lax.all_to_all(
        send_rows, "expert", split_axis=0, concat_axis=0, tiled=True
    ).reshape(slot_count, width_part)

    def gate_up_step(offset, length, current):
        gate_acc = rounded(jnp.dot(expert_rows, w_gate, preferred_element_type=jnp.float32))
        up_acc = rounded(jnp.dot(expert_rows, w_up, preferred_element_type=jnp.float32))
        return (gate_acc, up_acc)

    zero_hidden = jnp.zeros((slot_count, hidden_units), jnp.float32)
    gate_part, up_part = run_blocks(gate_up_step, (zero_hidden, zero_hidden))
    gate_pre, up_pre = (
        lax.psum(gate_part.astype(jnp.bfloat16), "dp").astype(jnp.float32),
        lax.psum(up_part.astype(jnp.bfloat16), "dp").astype(jnp.float32),
    )
    hidden = (jax.nn.silu(gate_pre) * up_pre).astype(jnp.bfloat16)

    def down_step(offset, length, current):
        result_rows = jnp.dot(hidden, w_down, preferred_element_type=jnp.float32).astype(
            jnp.bfloat16
        )
        return result_rows

    expert_out = run_blocks(down_step, jnp.zeros((slot_count, width_part), jnp.bfloat16))
    returned = send_back(expert_out.reshape(groups, capacity, width_part)).reshape(
        slot_count, width_part
    )
    pair_out = returned[slot_of_pair].reshape(tok_rows, top_count, width_part)
    layer_out = jnp.sum(weights[:, :, None] * pair_out.astype(jnp.float32), axis=1).astype(
        jnp.bfloat16
    )
    pair_grad = (
        (weights[:, :, None] * out_grad[:, None, :].astype(jnp.float32))
        .astype(jnp.bfloat16)
        .reshape(pair_count, width_part)
    )
    send_grads = jnp.concatenate([pair_grad, zero_row], axis=0)[pair_of_slot].reshape(
        groups, capacity, width_part
    )
    grad_rows = lax.all_to_all(
        send_grads, "expert", split_axis=0, concat_axis=0, tiled=True
    ).reshape(slot_count, width_part)

    def hidden_grad_step(offset, length, current):
        hidden_acc = rounded(contract_last(grad_rows, w_down))
        down_acc = contract_rows(hidden, grad_rows)
        return (hidden_acc, down_acc)

    hidden_grad_part, down_total = run_blocks(
        hidden_grad_step, (zero_hidden, jnp.zeros((hidden_units, width_part), jnp.float32))
    )
    hidden_grad = lax.psum(hidden_grad_part.astype(jnp.bfloat16), "dp").astype(jnp.float32)
    gate_pre_grad, up_pre_grad = swish_grads(hidden_grad, gate_pre, up_pre)

    def token_step(offset, length, current):
        pair_token = (
            contract_last(gate_pre_grad, w_gate) + contract_last(up_pre_grad, w_up)
        ).astype(jnp.bfloat16)
        gate_acc = contract_rows(expert_rows, gate_pre_grad)
        up_acc = contract_rows(expert_rows, up_pre_grad)
        return (pair_token, gate_acc, up_acc)

    zero_weight = jnp.zeros((width_part, hidden_units), jnp.float32)
    token_part, gate_total, up_total = run_blocks(
        token_step, (jnp.zeros((slot_count, width_part), jnp.bfloat16), zero_weight, zero_weight)
    )
    returned_grad = send_back(token_part.reshape(groups, capacity, width_part)).reshape(
        slot_count, width_part
    )
    pair_token_grad = returned_grad[slot_of_pair].reshape(tok_rows, top_count, width_part)
    token_grad = jnp.sum(pair_token_grad.astype(jnp.float32), axis=1).astype(jnp.bfloat16)
    return (
        layer_out,
        token_grad,
        gate_total.astype(jnp.bfloat16)[None],
        up_total.astype(jnp.bfloat16)[None],
        down_total.astype(jnp.bfloat16)[None],
    )


def solution(mesh):
    placed = (
        P("expert", "dp"),
        P("expert", None),
        P("expert", None),
        P("expert", "dp", None),
        P("expert", "dp", None),
        P("expert", None, "dp"),
        P("expert", "dp"),
    )
    return jax.shard_map(
        body,
        mesh=mesh,
        in_specs=placed,
        out_specs=(
            P("expert", "dp"),
            P("expert", "dp"),
            P("expert", "dp", None),
            P("expert", "dp", None),
            P("expert", None, "dp"),
        ),
        check_vma=False,
    )
```

profile of v0, /device:TPU:17, one launch (start us, length us, event | category | flops | bytes accessed | tf_op | source)
XLA Modules:
  0.0 307.3 jit_solution(5502696387443109241)
XLA Ops:
  13.0 3.4 %scatter_custom_fusion = s32[768]{0:T(1024)S(1)} fusion(s32[768]{0:T(1024)S(1)} %fusion.38, s32[768]{0:T(1024)S(1)} %iota.11, s32[]{:T(128)} %constant.30.clone.1), kind=kCustom, calls=%fused_computation.67 | custom fusion | bytes 3076 | tf_op jit(solution)/shard_map/scatter | solution.py:56
  17.8 3.6 %gather_fusion.2 = bf16[768,1024]{1,0:T(8,128)(2,1)} fusion(bf16[769,1024]{1,0:T(8,128)(2,1)S(1)} %concatenate.7, s32[1024]{0:T(1024)S(1)} %get-tuple-element.10), kind=kCustom, calls=%fused_computation.2 | custom fusion | bytes 3148800 | tf_op jit(solution)/shard_map/gather | solution.py:103
  21.4 5.5 %all-to-all-start.2 = ((bf16[8,96,1024]{2,1,0:T(8,128)(2,1)}), bf16[8,96,1024]{2,1,0:T(8,128)(2,1)S(1)}, u32[]{:S(2)}, u32[]{:S(2)}) async-start(bf16[8,96,1024]{2,1,0:T(8,128)(2,1)} %bitcast.64), calls=%async_computation.2 | async-start | bytes 3145728 | tf_op jit(solution)/shard_map/all_to_all | solution.py:106
  27.8 3.6 %gather_fusion = bf16[768,1024]{1,0:T(8,128)(2,1)} fusion(bf16[97,1024]{1,0:T(8,128)(2,1)S(1)} %concatenate.6, s32[1024]{0:T(1024)S(1)} %get-tuple-element.11), kind=kCustom, calls=%fused_computation | custom fusion | bytes 3148800 | tf_op jit(solution)/shard_map/gather | solution.py:60
  31.4 29.5 %all-to-all-done.2 = bf16[8,96,1024]{2,1,0:T(8,128)(2,1)S(1)} async-done(((bf16[8,96,1024]{2,1,0:T(8,128)(2,1)}), bf16[8,96,1024]{2,1,0:T(8,128)(2,1)S(1)}, u32[]{:S(2)}, u32[]{:S(2)}) %all-to-all-start.2) | async-done | bytes 1572896 | tf_op jit(solution)/shard_map/all_to_all | solution.py:106
  60.9 8.0 %all-to-all-start = ((bf16[8,96,1024]{2,1,0:T(8,128)(2,1)}), bf16[8,96,1024]{2,1,0:T(8,128)(2,1)}, u32[]{:S(2)}, u32[]{:S(2)}) async-start(bf16[8,96,1024]{2,1,0:T(8,128)(2,1)} %bitcast.3), calls=%async_computation | async-start | bytes 3145728 | tf_op jit(solution)/shard_map/all_to_all | solution.py:67
  68.9 2.4 fusion.27
  71.3 31.6 %all-to-all-done = bf16[8,96,1024]{2,1,0:T(8,128)(2,1)} async-done(((bf16[8,96,1024]{2,1,0:T(8,128)(2,1)}), bf16[8,96,1024]{2,1,0:T(8,128)(2,1)}, u32[]{:S(2)}, u32[]{:S(2)}) %all-to-all-start) | async-done | bytes 1572896 | tf_op jit(solution)/shard_map/all_to_all | solution.py:67
  102.9 4.4 %fusion.24 = bf16[768,768]{1,0:T(8,128)(2,1)} fusion(bf16[768,1024]{1,0:T(8,128)(2,1)} %bitcast.4, bf16[1,1024,768]{2,1,0:T(8,128)(2,1)} %param.11), kind=kOutput, calls=%fused_computation.41 | convolution fusion | flops 1208549376 | bytes 4325376 | tf_op jit(solution)/shard_map/dot_general | solution.py:73
  107.3 3.8 %fusion.21 = bf16[768,768]{1,0:T(8,128)(2,1)} fusion(bf16[768,1024]{1,0:T(8,128)(2,1)} %bitcast.4, bf16[1,1024,768]{2,1,0:T(8,128)(2,1)S(1)} %copy-done.9), kind=kOutput, calls=%fused_computation.40 | convolution fusion | flops 1208549376 | bytes 4325376 | tf_op jit(solution)/shard_map/dot_general | solution.py:72
  111.2 96.3 %all-reduce.5.cloned.1.call-done = (bf16[768,768]{1,0:T(8,128)(2,1)}, bf16[768,768]{1,0:T(8,128)(2,1)}, bf16[768,768]{1,0:T(8,128)(2,1)}) async-done(((bf16[768,768]{1,0:T(8,128)(2,1)}, bf16[768,768]{1,0:T(8,128)(2,1)}, bf16[768,768]{1,0:T(8,128)(2,1)}), (bf16[768,768]{1,0:T(8,128)(2,1)}, bf16[768,768]{1,0:T(8,128)(2,1)}, bf16[768,768]{1,0:T(8,128)(2,1)})) %all-reduce.5.cloned.1.call-update) | async-done | bytes 3538960 | tf_op jit(solution)/shard_map/psum | solution.py:80
  207.5 4.3 %convolution_convert_fusion.3 = bf16[768,1024]{1,0:T(8,128)(2,1)} fusion(bf16[1,768,1024]{2,1,0:T(8,128)(2,1)S(1)} %copy-done, bf16[768,768]{1,0:T(8,128)(2,1)} %get-tuple-element.5, bf16[768,768]{1,0:T(8,128)(2,1)} %get-tuple-element.6), kind=kOutput, calls=%fused_computation.28 | convolution fusion | flops 1213464576 | bytes 5505024 | tf_op jit(solution)/shard_map/dot_general | solution.py:85
  211.8 5.4 %all-to-all-start.1 = ((bf16[8,96,1024]{2,1,0:T(8,128)(2,1)}), bf16[8,96,1024]{2,1,0:T(8,128)(2,1)S(1)}, u32[]{:S(2)}, u32[]{:S(2)}) async-start(bf16[8,96,1024]{2,1,0:T(8,128)(2,1)} %bitcast.68), calls=%async_computation.1 | async-start | bytes 3145728 | tf_op jit(solution)/shard_map/all_to_all | solution.py:33
  217.2 3.2 %fusion.5 = bf16[768,768]{1,0:T(8,128)(2,1)S(1)} fusion(bf16[768,768]{1,0:T(8,128)(2,1)} %get-tuple-element.5, bf16[768,768]{1,0:T(8,128)(2,1)} %get-tuple-element.7, bf16[768,768]{1,0:T(8,128)(2,1)} %get-tuple-element.6), kind=kLoop, calls=%fused_computation.19 | loop fusion | flops 7667712 | bytes 4718592 | tf_op jit(solution)/shard_map/convert_element_type | solution.py:27
  223.6 2.7 add_convert_fusion
  226.4 24.9 %all-to-all-done.1 = bf16[8,96,1024]{2,1,0:T(8,128)(2,1)S(1)} async-done(((bf16[8,96,1024]{2,1,0:T(8,128)(2,1)}), bf16[8,96,1024]{2,1,0:T(8,128)(2,1)S(1)}, u32[]{:S(2)}, u32[]{:S(2)}) %all-to-all-start.1) | async-done | bytes 1572896 | tf_op jit(solution)/shard_map/all_to_all | solution.py:33
  251.3 8.0 %all-to-all-start.3 = ((bf16[8,96,1024]{2,1,0:T(8,128)(2,1)}), bf16[8,96,1024]{2,1,0:T(8,128)(2,1)}, u32[]{:S(2)}, u32[]{:S(2)}) async-start(bf16[8,96,1024]{2,1,0:T(8,128)(2,1)} %bitcast.67), calls=%async_computation.3 | async-start | bytes 3145728 | tf_op jit(solution)/shard_map/all_to_all | solution.py:33
  259.3 4.5 %fusion.30 = bf16[1,1024,768]{2,1,0:T(8,128)(2,1)} fusion(bf16[768,1024]{1,0:T(8,128)(2,1)} %bitcast.4, bf16[768,768]{1,0:T(8,128)(2,1)} %copy-done.8), kind=kOutput, calls=%fused_computation.43 | convolution fusion | flops 1208745984 | bytes 4325376 | tf_op jit(solution)/shard_map/dot_general | solution.py:18
  263.8 2.7 fusion.32
  266.5 4.2 %fusion.31 = bf16[1,1024,768]{2,1,0:T(8,128)(2,1)} fusion(bf16[768,1024]{1,0:T(8,128)(2,1)} %bitcast.4, bf16[768,768]{1,0:T(8,128)(2,1)S(1)} %copy-done.6, bf16[768,768]{1,0:T(8,128)(2,1)S(1)} %copy-done.4), kind=kOutput, calls=%fused_computation.44 | convolution fusion | flops 1213464576 | bytes 5505024 | tf_op jit(solution)/shard_map/dot_general | solution.py:18
  270.7 3.5 %gather_fusion.1 = bf16[768,1024]{1,0:T(8,128)(2,1)} fusion(bf16[768,1024]{1,0:T(8,128)(2,1)S(1)} %bitcast.63, s32[1024]{0:T(1024)S(1)} %pad_clamp_fusion.1), kind=kCustom, calls=%fused_computation.1 | custom fusion | bytes 3148800 | tf_op jit(solution)/shard_map/gather | solution.py:94
  274.3 3.1 %fusion = bf16[96,1024]{1,0:T(8,128)(2,1)} fusion(bf16[768,1024]{1,0:T(8,128)(2,1)} %gather_fusion.1, f32[96,8]{1,0:T(8,128)S(1)} %copy.15), kind=kLoop, calls=%fused_computation.9 | loop fusion | flops 2260992 | bytes 1772544 | tf_op jit(solution)/shard_map/reduce_sum | solution.py:95
  277.4 15.9 %all-to-all-done.3 = bf16[8,96,1024]{2,1,0:T(8,128)(2,1)} async-done(((bf16[8,96,1024]{2,1,0:T(8,128)(2,1)}), bf16[8,96,1024]{2,1,0:T(8,128)(2,1)}, u32[]{:S(2)}, u32[]{:S(2)}) %all-to-all-start.3) | async-done | bytes 1572896 | tf_op jit(solution)/shard_map/all_to_all | solution.py:33
  293.3 5.4 %gather_fusion.3 = bf16[768,1024]{1,0:T(8,128)(2,1)S(1)} fusion(bf16[768,1024]{1,0:T(8,128)(2,1)} %bitcast.15, s32[1024]{0:T(1024)S(1)} %pad_clamp_fusion.1), kind=kCustom, calls=%fused_computation.3 | custom fusion | bytes 3148800 | tf_op jit(solution)/shard_map/gather | solution.py:136
  (54 shorter events, 13.1 us)
Async XLA Ops:
  7.2 61.7 %copy-start = (bf16[1,768,1024]{2,1,0:T(8,128)(2,1)S(1)}, bf16[1,768,1024]{2,1,0:T(8,128)(2,1)}, u32[]{:S(2)}) copy-start(bf16[1,768,1024]{2,1,0:T(8,128)(2,1)} %param.12) | copy-start | bytes 4718596
  21.4 39.6 %all-to-all-start.2 = ((bf16[8,96,1024]{2,1,0:T(8,128)(2,1)}), bf16[8,96,1024]{2,1,0:T(8,128)(2,1)S(1)}, u32[]{:S(2)}, u32[]{:S(2)}) async-start(bf16[8,96,1024]{2,1,0:T(8,128)(2,1)} %bitcast.64), calls=%async_computation.2 | async-start | bytes 3145728 | tf_op jit(solution)/shard_map/all_to_all | solution.py:106
  60.9 8.0 %copy-start.1 = (bf16[8,96,1024]{2,1,0:T(8,128)(2,1)}, bf16[8,96,1024]{2,1,0:T(8,128)(2,1)S(1)}, u32[]{:S(2)}) copy-start(bf16[8,96,1024]{2,1,0:T(8,128)(2,1)S(1)} %all-to-all-done.2) | copy-start | bytes 4718596
  60.9 42.0 %all-to-all-start = ((bf16[8,96,1024]{2,1,0:T(8,128)(2,1)}), bf16[8,96,1024]{2,1,0:T(8,128)(2,1)}, u32[]{:S(2)}, u32[]{:S(2)}) async-start(bf16[8,96,1024]{2,1,0:T(8,128)(2,1)} %bitcast.3), calls=%async_computation | async-start | bytes 3145728 | tf_op jit(solution)/shard_map/all_to_all | solution.py:67
  68.9 138.6 %all-reduce.5.cloned.1.call-start = ((), (), s32[]{:S(2)}) async-start(), calls=%async_computation.4 | async-start | bytes 7077888 | tf_op jit(solution)/shard_map/psum | solution.py:80
  102.9 4.4 %copy-start.9 = (bf16[1,1024,768]{2,1,0:T(8,128)(2,1)S(1)}, bf16[1,1024,768]{2,1,0:T(8,128)(2,1)}, u32[]{:S(2)}) copy-start(bf16[1,1024,768]{2,1,0:T(8,128)(2,1)} %param.10) | copy-start | bytes 4718596
  211.8 39.5 %all-to-all-start.1 = ((bf16[8,96,1024]{2,1,0:T(8,128)(2,1)}), bf16[8,96,1024]{2,1,0:T(8,128)(2,1)S(1)}, u32[]{:S(2)}, u32[]{:S(2)}) async-start(bf16[8,96,1024]{2,1,0:T(8,128)(2,1)} %bitcast.68), calls=%async_computation.1 | async-start | bytes 3145728 | tf_op jit(solution)/shard_map/all_to_all | solution.py:33
  217.2 4.3 %copy-start.10 = (bf16[1,1024,768]{2,1,0:T(8,128)(2,1)S(1)}, bf16[1,1024,768]{2,1,0:T(8,128)(2,1)}, u32[]{:S(2)}) copy-start(bf16[1,1024,768]{2,1,0:T(8,128)(2,1)} %param.10) | copy-start | bytes 4718596
  220.4 1.1 copy-start.8
  221.5 1.4 copy-start.3
  221.5 1.6 copy-start.5
  221.5 2.1 copy-start.11
  251.3 42.0 %all-to-all-start.3 = ((bf16[8,96,1024]{2,1,0:T(8,128)(2,1)}), bf16[8,96,1024]{2,1,0:T(8,128)(2,1)}, u32[]{:S(2)}, u32[]{:S(2)}) async-start(bf16[8,96,1024]{2,1,0:T(8,128)(2,1)} %bitcast.67), calls=%async_computation.3 | async-start | bytes 3145728 | tf_op jit(solution)/shard_map/all_to_all | solution.py:33
  259.3 4.5 %copy-start.2 = (bf16[8,96,1024]{2,1,0:T(8,128)(2,1)S(1)}, bf16[8,96,1024]{2,1,0:T(8,128)(2,1)}, u32[]{:S(2)}) copy-start(bf16[8,96,1024]{2,1,0:T(8,128)(2,1)} %copy-done.1) | copy-start | bytes 4718596
  259.3 4.5 %copy-start.4 = (bf16[768,768]{1,0:T(8,128)(2,1)S(1)}, bf16[768,768]{1,0:T(8,128)(2,1)}, u32[]{:S(2)}) copy-start(bf16[768,768]{1,0:T(8,128)(2,1)} %get-tuple-element.6) | copy-start | bytes 3538948
  259.3 4.5 %copy-start.7 = (bf16[768,768]{1,0:T(8,128)(2,1)S(1)}, bf16[768,768]{1,0:T(8,128)(2,1)}, u32[]{:S(2)}) copy-start(bf16[768,768]{1,0:T(8,128)(2,1)} %get-tuple-element.5) | copy-start | bytes 3538948
  263.8 2.7 copy-start.6
Sparse Core Ops, SparseCore 0:
  111.3 96.1 all-reduce.4
where the time goes:
time: 313 us; the launch traced here: 307 us
  waiting for transfers between devices  198 us (63%)
  matrix products  30.5 us (10%)
  starting transfers between devices  26.9 us (9%)
  local copies, waits for them, and re-layouts  24 us (8%)
  between operations  14.2 us (5%)
  other arithmetic  13.4 us (4%)
    psum x1, waiting for transfers between devices, body(): lax.psum(up_part.astype(jnp.bfloat16), 'dp').astype(jnp.float32)  96.3 us
    all_to_all x2, waiting for transfers between devices, send_back(): lax.all_to_all(values, 'expert', split_axis=0, concat_axis=0, tiled=True)  40.9 us
    all_to_all x1, waiting for transfers between devices, body(): lax.all_to_all(send_rows, 'expert', split_axis=0, concat_axis=0, tiled=True)  31.6 us
    all_to_all x1, waiting for transfers between devices, body(): lax.all_to_all(send_grads, 'expert', split_axis=0, concat_axis=0, tiled=T...  29.5 us
    all_to_all x2, starting transfers between devices, send_back(): lax.all_to_all(values, 'expert', split_axis=0, concat_axis=0, tiled=True)  13.4 us
    dot_general x3, matrix products, contract_rows(): lax.dot_general(first_op, second_op, (((0,), (0,)), ((), ())), preferred_...  11.4 us
    all_to_all x1, starting transfers between devices, body(): lax.all_to_all(send_rows, 'expert', split_axis=0, concat_axis=0, tiled=True)  7.96 us
    dot_general x3, matrix products, contract_last(): lax.dot_general(first_op, second_op, (((1,), (1,)), ((), ())), preferred_...  6.56 us
  transfers between devices with their start and end apart: 5, of which 5 were waited for; matrix products, arithmetic and copies ran while one was open for 11% of the time, Pallas kernels for 0%

commit v1 on v0

--- a/solution.py
+++ b/solution.py
@@ -33,7 +33,7 @@
     return lax.all_to_all(values, "expert", split_axis=0, concat_axis=0, tiled=True)
 
 
-def body(tokens, expert_ids, gate_probs, gate_weight, up_weight, down_weight, out_grad):
+def sparse_body(tokens, expert_ids, gate_probs, gate_weight, up_weight, down_weight, out_grad):
     tok_rows, width_part = tokens.shape
     top_count = expert_ids.shape[1]
     groups = lax.axis_size("expert")
@@ -144,6 +144,53 @@
     )
 
 
+def dense_body(tokens, expert_ids, gate_probs, gate_weight, up_weight, down_weight, out_grad):
+    groups = lax.axis_size("expert")
+    me = lax.axis_index("expert")
+    w_gate = gate_weight[0]
+    w_up = up_weight[0]
+    w_down = down_weight[0]
+    weights = gate_probs / jnp.sum(gate_probs, axis=1, keepdims=True)
+    named = expert_ids[:, :, None] == jnp.arange(groups, dtype=jnp.int32)[None, None, :]
+    by_expert = jnp.sum(jnp.where(named, weights[:, :, None], 0.0), axis=1)
+    all_weights = lax.all_gather(by_expert, "expert", axis=0, tiled=True)
+    mine = jnp.arange(groups, dtype=jnp.int32)[None, :] == me
+    weight = jnp.sum(jnp.where(mine, all_weights, 0.0), axis=1, keepdims=True)
+    rows = lax.all_gather(tokens, "expert", axis=0, tiled=True)
+    grads = lax.all_gather(out_grad, "expert", axis=0, tiled=True)
+    pair_grad = (weight * grads.astype(jnp.float32)).astype(jnp.bfloat16)
+
+    def total(values):
+        return lax.psum(values.astype(jnp.bfloat16), "dp").astype(jnp.float32)
+
+    gate_pre = total(jnp.dot(rows, w_gate, preferred_element_type=jnp.float32))
+    up_pre = total(jnp.dot(rows, w_up, preferred_element_type=jnp.float32))
+    hidden_grad = total(contract_last(pair_grad, w_down))
+    hidden = (jax.nn.silu(gate_pre) * up_pre).astype(jnp.bfloat16)
+    expert_out = jnp.dot(hidden, w_down, preferred_element_type=jnp.float32)
+    layer_out = lax.psum_scatter(
+        (weight * expert_out).astype(jnp.bfloat16), "expert", scatter_dimension=0, tiled=True
+    )
+    gate_pre_grad, up_pre_grad = swish_grads(hidden_grad, gate_pre, up_pre)
+    pair_token = contract_last(gate_pre_grad, w_gate) + contract_last(up_pre_grad, w_up)
+    token_grad = lax.psum_scatter(
+        pair_token.astype(jnp.bfloat16), "expert", scatter_dimension=0, tiled=True
+    )
+    return (
+        layer_out,
+        token_grad,
+        contract_rows(rows, gate_pre_grad).astype(jnp.bfloat16)[None],
+        contract_rows(rows, up_pre_grad).astype(jnp.bfloat16)[None],
+        contract_rows(hidden, pair_grad).astype(jnp.bfloat16)[None],
+    )
+
+
+def body(tokens, expert_ids, *rest):
+    if expert_ids.shape[1] == lax.axis_size("expert"):
+        return dense_body(tokens, expert_ids, *rest)
+    return sparse_body(tokens, expert_ids, *rest)
+
+
 def solution(mesh):
     placed = (
         P("expert", "dp"),

time: 313 us -> 242 us (0.77)
  the two profiles are of different devices: /device:TPU:17 before, /device:TPU:0 now
where the time goes in v1:
time: 242 us; the launch traced here: 241 us
  waiting for transfers between devices  169 us (70%)
  matrix products  31.2 us (13%)
  blocking collectives  15.7 us (6%)
  between operations  13.9 us (6%)
  local copies, waits for them, and re-layouts  6.11 us (3%)
  other arithmetic  5 us (2%)
    psum x1, waiting for transfers between devices, total(): return lax.psum(values.astype(jnp.bfloat16), 'dp').astype(jnp.float32)  93.8 us
    reduce_scatter x1, waiting for transfers between devices, dense_body(): lax.psum_scatter(pair_token.astype(jnp.bfloat16), 'expert', scatter_dimen...  34.8 us
    all_gather x1, waiting for transfers between devices, dense_body(): grads = lax.all_gather(out_grad, 'expert', axis=0, tiled=True)  19.2 us
    all_gather x1, blocking collectives, dense_body(): all_weights = lax.all_gather(by_expert, 'expert', axis=0, tiled=True)  15.7 us
    dot_general x3, matrix products, contract_rows(): lax.dot_general(first_op, second_op, (((0,), (0,)), ((), ())), preferred_...  12 us
    all_gather x1, waiting for transfers between devices, dense_body(): rows = lax.all_gather(tokens, 'expert', axis=0, tiled=True)  10.8 us
    reduce_scatter x1, waiting for transfers between devices, dense_body(): lax.psum_scatter((weight * expert_out).astype(jnp.bfloat16), 'expert', sc...  8.91 us
    dot_general x3, matrix products, contract_last(): lax.dot_general(first_op, second_op, (((1,), (1,)), ((), ())), preferred_...  8.01 us
  transfers between devices with their start and end apart: 5, of which 5 were waited for; matrix products, arithmetic and copies ran while one was open for 13% of the time, Pallas kernels for 0%

profile of v1, /device:TPU:0, one launch (start us, length us, event | category | flops | bytes accessed | tf_op | source)
XLA Modules:
  0.0 241.2 jit_solution(16957649568953272035)
XLA Ops:
  8.0 0.7 all-gather.6.cloned.1.call-update
  8.7 0.7 reduce_sum.27
  9.4 0.7 broadcast_divide_fusion
  10.1 0.7 select_reduce_fusion
  10.8 15.7 %all-gather = f32[8,96,8]{1,2,0:T(8,128)S(1)} all-gather(f32[1,96,8]{1,2,0:T(8,128)S(1)} %bitcast.40), channel_id=1, replica_groups=mesh['dp'=4,'expert'=8] {'expert'}, dimensions={0}, use_global_device_ids=true | all-gather | bytes 27648 | tf_op jit(solution)/shard_map/all_gather | solution.py:156
  26.7 10.8 %all-gather.4.cloned.1.call-done = bf16[768,1024]{1,0:T(8,128)(2,1)} async-done(((bf16[96,1024]{1,0:T(8,128)(2,1)}), bf16[768,1024]{1,0:T(8,128)(2,1)}) %all-gather.4.cloned.1.call-update) | async-done | bytes 1572880 | tf_op jit(solution)/shard_map/all_gather | solution.py:159
  37.5 4.4 %fusion.22 = bf16[768,768]{1,0:T(8,128)(2,1)} fusion(bf16[768,1024]{1,0:T(8,128)(2,1)} %all-gather.4.cloned.1.call-done, bf16[1,1024,768]{2,1,0:T(8,128)(2,1)} %param.11), kind=kOutput, calls=%fused_computation.32 | convolution fusion | flops 1208549376 | bytes 4325376 | tf_op jit(solution)/shard_map/dot_general | solution.py:167
  41.9 2.4 fusion.19
  44.3 19.2 %all-gather.6.cloned.1.call-done = bf16[768,1024]{1,0:T(8,128)(2,1)} async-done(((bf16[96,1024]{1,0:T(8,128)(2,1)}), bf16[768,1024]{1,0:T(8,128)(2,1)}) %all-gather.6.cloned.1.call-update) | async-done | bytes 1572880 | tf_op jit(solution)/shard_map/all_gather | solution.py:160
  63.5 3.9 %fusion.25 = bf16[768,768]{1,0:T(8,128)(2,1)} fusion(bf16[1,768,1024]{2,1,0:T(8,128)(2,1)S(1)} %copy-done, bf16[768,1024]{1,0:T(8,128)(2,1)} %all-gather.6.cloned.1.call-done, f32[768]{0:T(1024)S(1)} %select_reduce_fusion.1), kind=kOutput, calls=%fused_computation.33 | convolution fusion | flops 1210908672 | bytes 4328448 | tf_op jit(solution)/shard_map/dot_general | solution.py:12
  67.4 93.8 %all-reduce.3.cloned.1.call-done = (bf16[768,768]{1,0:T(8,128)(2,1)}, bf16[768,768]{1,0:T(8,128)(2,1)}, bf16[768,768]{1,0:T(8,128)(2,1)}) async-done(((bf16[768,768]{1,0:T(8,128)(2,1)}, bf16[768,768]{1,0:T(8,128)(2,1)}, bf16[768,768]{1,0:T(8,128)(2,1)}), (bf16[768,768]{1,0:T(8,128)(2,1)}, bf16[768,768]{1,0:T(8,128)(2,1)}, bf16[768,768]{1,0:T(8,128)(2,1)})) %all-reduce.3.cloned.1.call-update) | async-done | bytes 3538960 | tf_op jit(solution)/shard_map/psum | solution.py:164
  161.3 4.4 %multiply_convert_fusion.1 = bf16[768,1024]{1,0:T(8,128)(2,1)} fusion(bf16[1,768,1024]{2,1,0:T(8,128)(2,1)S(1)} %copy-done, f32[768]{0:T(1024)S(1)} %select_reduce_fusion.1, bf16[768,768]{1,0:T(8,128)(2,1)} %get-tuple-element.25, bf16[768,768]{1,0:T(8,128)(2,1)} %get-tuple-element.26), kind=kOutput, calls=%fused_computation.5 | convolution fusion | flops 1214251008 | bytes 5508096 | tf_op jit(solution)/shard_map/dot_general | solution.py:170
  165.9 1.0 copy-done.1
  166.9 2.8 %fusion.3 = bf16[768,768]{1,0:T(8,128)(2,1)S(1)} fusion(bf16[768,768]{1,0:T(8,128)(2,1)S(1)} %copy-done.1, bf16[768,768]{1,0:T(8,128)(2,1)} %get-tuple-element.27, bf16[768,768]{1,0:T(8,128)(2,1)} %get-tuple-element.26), kind=kLoop, calls=%fused_computation.12 | loop fusion | flops 7667712 | bytes 4718592 | tf_op jit(solution)/shard_map/convert_element_type | solution.py:27
  169.7 1.0 copy-done.4
  170.8 1.4 fusion.15
  173.0 2.7 %add_convert_fusion = bf16[768,1024]{1,0:T(8,128)(2,1)} fusion(f32[768,1024]{1,0:T(8,128)S(1)} %fusion.15, bf16[1,1024,768]{2,1,0:T(8,128)(2,1)S(1)} %copy-done.7, bf16[768,768]{1,0:T(8,128)(2,1)S(1)} %copy-done.3, bf16[768,768]{1,0:T(8,128)(2,1)S(1)} %copy-done.2), kind=kOutput, calls=%fused_computation.3 | convolution fusion | flops 1214251008 | bytes 8650752 | tf_op jit(solution)/shard_map/dot_general | solution.py:12
  175.8 3.7 %fusion.29 = bf16[1,1024,768]{1,2,0:T(8,128)(2,1)S(1)} fusion(bf16[768,1024]{1,0:T(8,128)(2,1)} %all-gather.4.cloned.1.call-done, bf16[768,768]{1,0:T(8,128)(2,1)} %get-tuple-element.27, bf16[768,768]{1,0:T(8,128)(2,1)} %get-tuple-element.26), kind=kOutput, calls=%fused_computation.35 | convolution fusion | flops 1213464576 | bytes 5505024 | tf_op jit(solution)/shard_map/dot_general | solution.py:18
  179.5 1.6 copy.27
  181.0 3.2 %fusion.28 = bf16[1,1024,768]{1,2,0:T(8,128)(2,1)S(1)} fusion(bf16[768,768]{1,0:T(8,128)(2,1)} %copy-done.4, bf16[768,1024]{1,0:T(8,128)(2,1)} %all-gather.4.cloned.1.call-done), kind=kOutput, calls=%fused_computation.34 | convolution fusion | flops 1208745984 | bytes 4325376 | tf_op jit(solution)/shard_map/dot_general | solution.py:18
  184.2 1.6 copy.26
  185.8 5.1 %fusion.30 = bf16[1,768,1024]{2,1,0:T(8,128)(2,1)} fusion(bf16[768,1024]{1,0:T(8,128)(2,1)} %all-gather.6.cloned.1.call-done, f32[768]{0:T(1024)S(1)} %select_reduce_fusion.1, bf16[768,768]{1,0:T(8,128)(2,1)} %get-tuple-element.25, bf16[768,768]{1,0:T(8,128)(2,1)} %get-tuple-element.26), kind=kOutput, calls=%fused_computation.36 | convolution fusion | flops 1215823872 | bytes 5508096 | tf_op jit(solution)/shard_map/dot_general | solution.py:18
  190.9 8.9 %reduce-scatter.3.cloned.1.call-done = bf16[96,1024]{1,0:T(8,128)(2,1)} async-done(((bf16[768,1024]{1,0:T(8,128)(2,1)}), bf16[96,1024]{1,0:T(8,128)(2,1)}) %reduce-scatter.3.cloned.1.call-update) | async-done | bytes 196624 | tf_op jit(solution)/shard_map/reduce_scatter | solution.py:171
  199.8 34.8 %reduce-scatter.5.cloned.1.call-done = bf16[96,1024]{1,0:T(8,128)(2,1)} async-done(((bf16[768,1024]{1,0:T(8,128)(2,1)}), bf16[96,1024]{1,0:T(8,128)(2,1)}) %reduce-scatter.5.cloned.1.call-update) | async-done | bytes 196624 | tf_op jit(solution)/shard_map/reduce_scatter | solution.py:176
  (29 shorter events, 2.1 us)
Async XLA Ops:
  7.2 56.3 %copy-start = (bf16[1,768,1024]{2,1,0:T(8,128)(2,1)S(1)}, bf16[1,768,1024]{2,1,0:T(8,128)(2,1)}, u32[]{:S(2)}) copy-start(bf16[1,768,1024]{2,1,0:T(8,128)(2,1)} %param.12) | copy-start | bytes 4718596
  7.2 30.3 %all-gather.4.cloned.1.call-start = ((), (), s32[]{:S(2)}) async-start(), calls=%async_computation.2 | async-start | bytes 1769472 | tf_op jit(solution)/shard_map/all_gather | solution.py:159
  7.9 55.6 %all-gather.6.cloned.1.call-start = ((), (), s32[]{:S(2)}) async-start(), calls=%async_computation.4 | async-start | bytes 1769472 | tf_op jit(solution)/shard_map/all_gather | solution.py:160
  8.7 152.6 %all-reduce.3.cloned.1.call-start = ((), (), s32[]{:S(2)}) async-start(), calls=%async_computation.6 | async-start | bytes 7077888 | tf_op jit(solution)/shard_map/psum | solution.py:164
  26.7 15.2 %copy-start.5 = (bf16[1,1024,768]{2,1,0:T(8,128)(2,1)S(1)}, bf16[1,1024,768]{2,1,0:T(8,128)(2,1)}, u32[]{:S(2)}) copy-start(bf16[1,1024,768]{2,1,0:T(8,128)(2,1)} %param.10) | copy-start | bytes 4718596
  37.5 4.4 %copy-start.8 = (bf16[768,1024]{1,0:T(8,128)(2,1)S(1)}, bf16[768,1024]{1,0:T(8,128)(2,1)}, u32[]{:S(2)}) copy-start(bf16[768,1024]{1,0:T(8,128)(2,1)} %all-gather.4.cloned.1.call-done) | copy-start | bytes 4718596
  67.4 132.4 %reduce-scatter.3.cloned.1.call-start = ((), (), s32[]{:S(2)}) async-start(), calls=%async_computation.3 | async-start | bytes 1769472 | tf_op jit(solution)/shard_map/reduce_scatter | solution.py:171
  165.6 1.3 copy-start.1
  165.7 69.0 %reduce-scatter.5.cloned.1.call-start = ((), (), s32[]{:S(2)}) async-start(), calls=%async_computation.5 | async-start | bytes 1769472 | tf_op jit(solution)/shard_map/reduce_scatter | solution.py:176
  166.9 3.8 %copy-start.6 = (bf16[1,1024,768]{2,1,0:T(8,128)(2,1)S(1)}, bf16[1,1024,768]{2,1,0:T(8,128)(2,1)}, u32[]{:S(2)}) copy-start(bf16[1,1024,768]{2,1,0:T(8,128)(2,1)} %param.10) | copy-start | bytes 4718596
  169.7 1.0 copy-start.4
  170.7 1.4 copy-start.2
  170.7 1.8 copy-start.3
  170.7 2.3 copy-start.7
Sparse Core Ops, SparseCore 0:
  9.7 27.7 all-gather.3
  39.1 24.3 all-gather.5
  67.5 93.6 all-reduce.2
  165.8 33.9 reduce-scatter.2
  202.5 32.0 reduce-scatter.4

commit v2 on v1

--- a/solution.py
+++ b/solution.py
@@ -1,6 +1,8 @@
 import jax
 import jax.numpy as jnp
 from jax import lax
+from jax.experimental import pallas as pl
+from jax.experimental.pallas import tpu as pltpu
 from jax.sharding import PartitionSpec as P
 
 
@@ -185,8 +187,316 @@
     )
 
 
+TILE = 256
+BLOCKS = 4
+PEERS = 4
+MESH = pl.DeviceIdType.MESH
+
+
+def layer_kernel(
+    tok_ref, grad_ref, wt_ref, wg_ref, wu_ref, wd_ref,
+    out_ref, tgrad_ref, gg_ref, ug_ref, dg_ref,
+    tok_all, grd_all, wt_all, wcol, pg_all,
+    gu_part, gu_in, hg_part, hg_in, gpre, upre, hid_all, dgu_all,
+    eo, eo_in, eo_sum, eo_z, tg, tg_in, tg_sum, tg_z,
+    tok_s, tok_r, grd_s, grd_r, tokf_s, grdf_s, wt_s, wt_r,
+    gu_s, gu_r, hg_s, hg_r, hid_s, hid_r, dgu_s, dgu_r,
+    eo_s, eo_r, eoz_s, eoz_r, tg_s, tg_r, tgz_s, tgz_r,
+):
+    dp = lax.axis_index("dp")
+    ex = lax.axis_index("expert")
+    z = ex // 2
+    c = ex % 2
+    oc = 1 - c
+    rows, width = tok_ref.shape
+    units = wg_ref.shape[1]
+    share = gu_part.shape[2]
+    both = 2 * rows
+    bf16 = jnp.bfloat16
+    f32 = jnp.float32
+
+    def block_at(step):
+        return ((z // 2 + step // 2) % 2) * 2 + (z + step) % 2
+
+    def peer_at(k):
+        return (dp + k) % PEERS
+
+    def remote(src, dst, send, recv, to_dp, to_ex):
+        return pltpu.make_async_remote_copy(
+            src_ref=src, dst_ref=dst, send_sem=send, recv_sem=recv,
+            device_id=(to_dp, to_ex), device_id_type=MESH,
+        )
+
+    barrier = pltpu.get_barrier_semaphore()
+    for k in range(1, 8):
+        pl.semaphore_signal(barrier, inc=1, device_id=(dp, (ex + k) % 8), device_id_type=MESH)
+    for k in range(1, PEERS):
+        pl.semaphore_signal(barrier, inc=1, device_id=(peer_at(k), ex), device_id_type=MESH)
+    pl.semaphore_wait(barrier, 10)
+
+    def own_copy(src, dst, send, recv, step):
+        if step == 0:
+            return remote(src, dst.at[z, c], send.at[0], recv.at[z, c], dp, z * 2 + oc)
+        return remote(src, dst.at[z, c], send.at[step], recv.at[z, c], dp, block_at(step) * 2 + c)
+
+    def hand_on(dst, send, recv, blk):
+        return remote(dst.at[blk, c], dst.at[blk, c], send.at[blk], recv.at[blk, c], dp, z * 2 + oc)
+
+    def arrived(dst, recv, send, blk, core):
+        remote(dst.at[blk, core], dst.at[blk, core], send.at[0], recv.at[blk, core], dp, z * 2 + oc).wait_recv()
+
+    def wt_copy(k):
+        return remote(wt_ref, wt_all.at[ex], wt_s.at[k], wt_r.at[ex], dp, (ex + k) % 8)
+
+    for step in range(4):
+        own_copy(tok_ref, tok_all, tok_s, tok_r, step).start()
+    for k in range(1, 8):
+        wt_copy(k).start()
+    tok_all[z, c] = tok_ref[...]
+    grd_all[z, c] = grad_ref[...]
+    wt_all[ex] = wt_ref[...]
+    own_copy(grad_ref, grd_all, grd_s, grd_r, 0).start()
+
+    def share_out(part, into, send, recv, blk, k):
+        to = peer_at(k)
+        return remote(part.at[blk, to], into.at[blk, dp], send.at[blk, k], recv.at[blk, dp], to, ex)
+
+    def spread(full, send, recv, blk, k):
+        return remote(full.at[blk, dp], full.at[blk, dp], send.at[blk, k], recv.at[blk, dp], peer_at(k), ex)
+
+    def landed(into, send, recv, blk):
+        for k in range(1, PEERS):
+            src = peer_at(k)
+            remote(into.at[blk, src], into.at[blk, src], send.at[blk, k], recv.at[blk, src], src, ex).wait_recv()
+
+    def gate_up(step):
+        blk = block_at(step)
+        if step > 0:
+            arrived(tok_all, tok_r, tok_s, blk, c)
+            hand_on(tok_all, tokf_s, tok_r, blk).start()
+            own_copy(grad_ref, grd_all, grd_s, grd_r, step).start()
+        arrived(tok_all, tok_r, tok_s, blk, oc)
+
+        @pl.loop(0, units // TILE)
+        def _(j):
+            cols = pl.ds(pl.multiple_of(j * TILE, TILE), TILE)
+            more = pl.ds(pl.multiple_of(units + j * TILE, TILE), TILE)
+            x = tok_all[blk].reshape(both, width)
+            gu_part[blk, :, :, cols] = jnp.dot(x, wg_ref[:, cols], preferred_element_type=f32).astype(bf16).reshape(PEERS, share, TILE)
+            gu_part[blk, :, :, more] = jnp.dot(x, wu_ref[:, cols], preferred_element_type=f32).astype(bf16).reshape(PEERS, share, TILE)
+
+        for k in range(1, PEERS):
+            share_out(gu_part, gu_in, gu_s, gu_r, blk, k).start()
+
+    for step in range(4):
+        gate_up(step)
+
+    for k in range(1, 8):
+        src = (ex + k) % 8
+        remote(wt_ref, wt_all.at[src], wt_s.at[k], wt_r.at[src], dp, src).wait_recv()
+    diagonal = lax.broadcasted_iota(jnp.int32, (128, 128), 0) == lax.broadcasted_iota(jnp.int32, (128, 128), 1)
+    for blk in range(4):
+        for core in range(2):
+            line = wt_all[blk * 2 + core, pl.ds(ex, 1), :]
+            column = jnp.sum(jnp.where(diagonal, line, 0.0), axis=1, keepdims=True)
+            wcol[blk, core] = jnp.broadcast_to(column[:rows], (rows, 128))
+
+    def hidden_grads(step):
+        blk = block_at(step)
+        if step > 0:
+            arrived(grd_all, grd_r, grd_s, blk, c)
+            hand_on(grd_all, grdf_s, grd_r, blk).start()
+        arrived(grd_all, grd_r, grd_s, blk, oc)
+        w = wcol[blk].reshape(both, 128)[:, :1]
+        pg_all[blk] = (w * grd_all[blk].reshape(both, width).astype(f32)).astype(bf16)
+
+        @pl.loop(0, units // TILE)
+        def _(j):
+            cols = pl.ds(pl.multiple_of(j * TILE, TILE), TILE)
+            part = contract_last(pg_all[blk], wd_ref[cols, :])
+            hg_part[blk, :, :, cols] = part.astype(bf16).reshape(PEERS, share, TILE)
+
+        for k in range(1, PEERS):
+            share_out(hg_part, hg_in, hg_s, hg_r, blk, k).start()
+
+    def make_hidden(step):
+        blk = block_at(step)
+        landed(gu_in, gu_s, gu_r, blk)
+        gu_in[blk, dp] = gu_part[blk, dp]
+        both_pre = jnp.sum(gu_in[blk].astype(f32), axis=0)
+        gate = both_pre[:, :units]
+        up = both_pre[:, units:]
+        gpre[blk] = gate
+        upre[blk] = up
+        hid_all[blk, dp] = (gate * jax.nn.sigmoid(gate) * up).astype(bf16)
+        for k in range(1, PEERS):
+            spread(hid_all, hid_s, hid_r, blk, k).start()
+
+    def make_grads(step):
+        blk = block_at(step)
+        landed(hg_in, hg_s, hg_r, blk)
+        hg_in[blk, dp] = hg_part[blk, dp]
+        hgrad = jnp.sum(hg_in[blk].astype(f32), axis=0)
+        gate = gpre[blk]
+        s = jax.nn.sigmoid(gate)
+        dgu_all[blk, dp, :, :units] = (hgrad * upre[blk] * s * (1.0 + gate * (1.0 - s))).astype(bf16)
+        dgu_all[blk, dp, :, units:] = (hgrad * (gate * s)).astype(bf16)
+        for k in range(1, PEERS):
+            spread(dgu_all, dgu_s, dgu_r, blk, k).start()
+
+    def to_partner(full, into, send, recv, blk):
+        return remote(full.at[blk, oc], into.at[blk], send.at[blk], recv.at[blk], dp, z * 2 + oc)
+
+    def home(total, into, send, recv, blk):
+        return remote(total.at[blk], into.at[z], send.at[blk], recv.at[z], dp, blk * 2 + c)
+
+    def expert_rows(step):
+        blk = block_at(step)
+        landed(hid_all, hid_s, hid_r, blk)
+        w = wcol[blk].reshape(both, 128)[:, :1]
+
+        @pl.loop(0, width // TILE)
+        def _(j):
+            cols = pl.ds(pl.multiple_of(j * TILE, TILE), TILE)
+            h = hid_all[blk].reshape(both, units)
+            part = jnp.dot(h, wd_ref[:, cols], preferred_element_type=f32).astype(bf16)
+            eo[blk, :, :, cols] = (w * part.astype(f32)).astype(bf16).reshape(2, rows, TILE)
+
+        to_partner(eo, eo_in, eo_s, eo_r, blk).start()
+
+    def token_rows(step):
+        blk = block_at(step)
+        landed(dgu_all, dgu_s, dgu_r, blk)
+
+        @pl.loop(0, width // TILE)
+        def _(j):
+            cols = pl.ds(pl.multiple_of(j * TILE, TILE), TILE)
+            part = contract_last(dgu_all[blk, :, :, :units].reshape(both, units), wg_ref[cols, :])
+            part += contract_last(dgu_all[blk, :, :, units:].reshape(both, units), wu_ref[cols, :])
+            tg[blk, :, :, cols] = part.astype(bf16).reshape(2, rows, TILE)
+
+        to_partner(tg, tg_in, tg_s, tg_r, blk).start()
+
+    def pair_sum(full, into, total, send, recv, zin, zsend, zrecv, step):
+        blk = block_at(step)
+        to_partner(full, into, send, recv, blk).wait_recv()
+        total[blk] = (full[blk, c].astype(f32) + into[blk].astype(f32)).astype(bf16)
+        if step > 0:
+            home(total, zin, zsend, zrecv, blk).start()
+
+    def finish(total, zin, zsend, zrecv, result):
+        for step in range(1, 4):
+            blk = block_at(step)
+            remote(total.at[blk], zin.at[blk], zsend.at[blk], zrecv.at[blk], dp, blk * 2 + c).wait_recv()
+        zin[z] = total[z]
+        result[...] = jnp.sum(zin[...].astype(f32), axis=0).astype(bf16)
+
+    order = (1, 2, 3, 0)
+    for step in range(4):
+        hidden_grads(step)
+        make_hidden(step)
+    for step in range(4):
+        make_grads(step)
+        expert_rows(step)
+    for step in order:
+        pair_sum(eo, eo_in, eo_sum, eo_s, eo_r, eo_z, eoz_s, eoz_r, step)
+
+    @pl.loop(0, units // TILE)
+    def _(j):
+        cols = pl.ds(pl.multiple_of(j * TILE, TILE), TILE)
+        h = hid_all[:, :, :, cols].reshape(BLOCKS * both, TILE)
+        dg_ref[cols, :] = contract_rows(h, pg_all[...].reshape(BLOCKS * both, width)).astype(bf16)
+
+    for step in range(4):
+        token_rows(step)
+        if step > 0:
+            pair_sum(tg, tg_in, tg_sum, tg_s, tg_r, tg_z, tgz_s, tgz_r, step - 1)
+    pair_sum(tg, tg_in, tg_sum, tg_s, tg_r, tg_z, tgz_s, tgz_r, 3)
+
+    @pl.loop(0, width // TILE)
+    def _(j):
+        cols = pl.ds(pl.multiple_of(j * TILE, TILE), TILE)
+        x = tok_all[:, :, :, cols].reshape(BLOCKS * both, TILE)
+        gg_ref[cols, :] = contract_rows(x, dgu_all[:, :, :, :units].reshape(BLOCKS * both, units)).astype(bf16)
+        ug_ref[cols, :] = contract_rows(x, dgu_all[:, :, :, units:].reshape(BLOCKS * both, units)).astype(bf16)
+
+    finish(eo_sum, eo_z, eoz_s, eoz_r, out_ref)
+    finish(tg_sum, tg_z, tgz_s, tgz_r, tgrad_ref)
+
+    for step in range(4):
+        blk = block_at(step)
+        own_copy(tok_ref, tok_all, tok_s, tok_r, step).wait_send()
+        own_copy(grad_ref, grd_all, grd_s, grd_r, step).wait_send()
+        if step > 0:
+            hand_on(tok_all, tokf_s, tok_r, blk).wait_send()
+            hand_on(grd_all, grdf_s, grd_r, blk).wait_send()
+            home(eo_sum, eo_z, eoz_s, eoz_r, blk).wait_send()
+            home(tg_sum, tg_z, tgz_s, tgz_r, blk).wait_send()
+        to_partner(eo, eo_in, eo_s, eo_r, blk).wait_send()
+        to_partner(tg, tg_in, tg_s, tg_r, blk).wait_send()
+        for k in range(1, PEERS):
+            share_out(gu_part, gu_in, gu_s, gu_r, blk, k).wait_send()
+            share_out(hg_part, hg_in, hg_s, hg_r, blk, k).wait_send()
+            spread(hid_all, hid_s, hid_r, blk, k).wait_send()
+            spread(dgu_all, dgu_s, dgu_r, blk, k).wait_send()
+    for k in range(1, 8):
+        wt_copy(k).wait_send()
+
+
+def kernel_body(tokens, expert_ids, gate_probs, gate_weight, up_weight, down_weight, out_grad):
+    rows, width = tokens.shape
+    units = gate_weight.shape[2]
+    share = 2 * rows // PEERS
+    weights = gate_probs / jnp.sum(gate_probs, axis=1, keepdims=True)
+    named = expert_ids[:, :, None] == jnp.arange(8, dtype=jnp.int32)[None, None, :]
+    by_expert = jnp.sum(jnp.where(named, weights[:, :, None], 0.0), axis=1)
+    lines = jnp.pad(by_expert.T, ((0, 0), (0, 128 - rows)))
+    bf16 = jnp.bfloat16
+    f32 = jnp.float32
+
+    def vm(*shape, dtype=bf16):
+        return pltpu.VMEM(shape, dtype)
+
+    def sem(*shape):
+        return pltpu.SemaphoreType.DMA(shape)
+
+    whole = pl.BlockSpec(memory_space=pltpu.VMEM)
+    shapes = [(rows, width), (rows, width), (width, units), (width, units), (units, width)]
+    flops = 2 * 9 * 8 * rows * width * units
+    results = pl.pallas_call(
+        layer_kernel,
+        out_shape=[jax.ShapeDtypeStruct(shape, bf16) for shape in shapes],
+        in_specs=[whole] * 6,
+        out_specs=[whole] * 5,
+        scratch_shapes=[
+            vm(4, 2, rows, width), vm(4, 2, rows, width), vm(8, 8, 128, dtype=f32),
+            vm(4, 2, rows, 128, dtype=f32), vm(4, 2 * rows, width),
+            vm(4, PEERS, share, 2 * units), vm(4, PEERS, share, 2 * units),
+            vm(4, PEERS, share, units), vm(4, PEERS, share, units),
+            vm(4, share, units, dtype=f32), vm(4, share, units, dtype=f32),
+            vm(4, PEERS, share, units), vm(4, PEERS, share, 2 * units),
+            vm(4, 2, rows, width), vm(4, rows, width), vm(4, rows, width), vm(4, rows, width),
+            vm(4, 2, rows, width), vm(4, rows, width), vm(4, rows, width), vm(4, rows, width),
+            sem(4), sem(4, 2), sem(4), sem(4, 2), sem(4), sem(4), sem(8), sem(8),
+            sem(4, 4), sem(4, 4), sem(4, 4), sem(4, 4), sem(4, 4), sem(4, 4), sem(4, 4), sem(4, 4),
+            sem(4), sem(4), sem(4), sem(4), sem(4), sem(4), sem(4), sem(4),
+        ],
+        compiler_params=pltpu.CompilerParams(
+            collective_id=0, has_side_effects=True, vmem_limit_bytes=56 * 1024 * 1024
+        ),
+        cost_estimate=pl.CostEstimate(flops=flops, bytes_accessed=12_000_000, transcendentals=0),
+        name="moe_layer",
+    )(tokens, out_grad, lines, gate_weight[0], up_weight[0], down_weight[0])
+    layer_out, token_grad, gate_grad, up_grad, down_grad = results
+    return layer_out, token_grad, gate_grad[None], up_grad[None], down_grad[None]
+
+
 def body(tokens, expert_ids, *rest):
-    if expert_ids.shape[1] == lax.axis_size("expert"):
+    groups = lax.axis_size("expert")
+    if expert_ids.shape[1] == groups:
+        fits = tokens.shape[0] % 32 == 0 and tokens.shape[0] <= 128
+        if groups == 8 and lax.axis_size("dp") == 4 and fits:
+            return kernel_body(tokens, expert_ids, *rest)
         return dense_body(tokens, expert_ids, *rest)
     return sparse_body(tokens, expert_ids, *rest)
 

time: 242 us -> 129 us (0.53)
  the two profiles are of different devices: /device:TPU:0 before, /device:TPU:17 now
where the time goes in v2:
time: 129 us
  Pallas kernels  116 us (90%)
  local copies, waits for them, and re-layouts  9.72 us (8%)
  other arithmetic  2.1 us (2%)
    pallas_call x1, Pallas kernels, kernel_body(): pl.pallas_call(layer_kernel, out_shape=[jax.ShapeDtypeStruct(shape, bf16)...  116 us
    unnamed x9, local copies, waits for them, and re-layouts  9.12 us

profile of v2, /device:TPU:17, one launch (start us, length us, event | category | flops | bytes accessed | tf_op | source)
XLA Modules:
  0.0 128.7 jit_solution(16706334234440152616)
XLA Ops:
  0.6 0.7 reduce_sum.18
  1.3 0.7 broadcast_divide_fusion
  2.0 0.7 select_reduce_fusion
  2.7 0.6 pad.4.wt_ref
  3.3 116.3 %moe_layer.1 = (bf16[96,1024]{1,0:T(8,128)(2,1)}, bf16[96,1024]{1,0:T(8,128)(2,1)}, bf16[1024,768]{1,0:T(8,128)(2,1)}, bf16[1024,768]{1,0:T(8,128)(2,1)}, bf16[768,1024]{1,0:T(8,128)(2,1)}) custom-call(bf16[96,1024]{1,0:T(8,128)(2,1)} %tok_ref.1, bf16[96,1024]{1,0:T(8,128)(2,1)} %grad_ref.1, f32[8,128]{1,0:T(8,128)} %pad.4.wt_ref, ...), custom_call_target="tpu_custom_call" | custom-call | flops 10871635968 | bytes 12000000 | tf_op jit(solution)/shard_map/moe_layer/pallas_call | solution.py:466
  119.6 1.6 %copy.19 = bf16[96,1024]{1,0:T(8,128)(2,1)} copy(bf16[96,1024]{1,0:T(8,128)(2,1)} %get-tuple-element.20) | data formatting | bytes 393216
  121.2 1.6 %copy.20 = bf16[96,1024]{1,0:T(8,128)(2,1)} copy(bf16[96,1024]{1,0:T(8,128)(2,1)} %get-tuple-element.21) | data formatting | bytes 393216
  122.8 0.0 copy-start.1
  122.8 2.8 %copy.21 = bf16[1,1024,768]{2,1,0:T(8,128)(2,1)} copy(bf16[1,1024,768]{2,1,0:T(8,128)(2,1)} %bitcast.9) | data formatting | bytes 3145728
  125.6 0.0 copy-done.1
  125.6 0.0 copy-start
  125.6 1.1 copy.22
  126.8 0.8 copy-done
  127.6 1.1 copy.23
Async XLA Ops:
  122.8 2.8 %copy-start.1 = (bf16[1024,768]{1,0:T(8,128)(2,1)S(1)}, bf16[1024,768]{1,0:T(8,128)(2,1)}, u32[]{:S(2)}) copy-start(bf16[1024,768]{1,0:T(8,128)(2,1)} %get-tuple-element.13) | copy-start | bytes 4718596
  125.6 2.0 %copy-start = (bf16[768,1024]{1,0:T(8,128)(2,1)S(1)}, bf16[768,1024]{1,0:T(8,128)(2,1)}, u32[]{:S(2)}) copy-start(bf16[768,1024]{1,0:T(8,128)(2,1)} %get-tuple-element.14) | copy-start | bytes 4718596

commit v3 on v2

--- a/solution.py
+++ b/solution.py
@@ -194,11 +194,15 @@
 
 
 def layer_kernel(
-    tok_ref, grad_ref, wt_ref, wg_ref, wu_ref, wd_ref,
-    out_ref, tgrad_ref, gg_ref, ug_ref, dg_ref,
-    tok_all, grd_all, wt_all, wcol, pg_all,
-    gu_part, gu_in, hg_part, hg_in, gpre, upre, hid_all, dgu_all,
+    tok_ref, grad_ref, ids_ref, probs_ref, wg_hbm, wu_hbm, wd_hbm,
+    out_ref, tgrad_ref, gg_hbm, ug_hbm, dg_hbm,
+    wg_ref, wu_ref, wd_ref, gg_ref, ug_ref, dg_ref,
+    tok_all, grd_all, wt_ref, wt_all, wcol, pg_all,
+    gu_part, gu_1x, gu_1y, gu_sx, gu_sy, gu_2x, gu_2y,
+    hg_part, hg_1x, hg_1y, hg_sx, hg_sy, hg_2x, hg_2y,
+    gpre, upre, hid_all, dgu_all,
     eo, eo_in, eo_sum, eo_z, tg, tg_in, tg_sum, tg_z,
+    w_s, g_s, d_s,
     tok_s, tok_r, grd_s, grd_r, tokf_s, grdf_s, wt_s, wt_r,
     gu_s, gu_r, hg_s, hg_r, hid_s, hid_r, dgu_s, dgu_r,
     eo_s, eo_r, eoz_s, eoz_r, tg_s, tg_r, tgz_s, tgz_r,
@@ -208,18 +212,27 @@
     z = ex // 2
     c = ex % 2
     oc = 1 - c
+    y = dp // 2
+    x = dp % 2
+    oy = 1 - y
+    ox = 1 - x
+    dp_x = y * 2 + ox
+    dp_y = oy * 2 + x
     rows, width = tok_ref.shape
     units = wg_ref.shape[1]
-    share = gu_part.shape[2]
+    share = gu_part.shape[3]
     both = 2 * rows
     bf16 = jnp.bfloat16
     f32 = jnp.float32
+    loads = [
+        pltpu.make_async_copy(src.at[0], dst, w_s.at[n])
+        for n, (src, dst) in enumerate(((wg_hbm, wg_ref), (wu_hbm, wu_ref), (wd_hbm, wd_ref)))
+    ]
+    for load in loads:
+        load.start()
 
     def block_at(step):
         return ((z // 2 + step // 2) % 2) * 2 + (z + step) % 2
-
-    def peer_at(k):
-        return (dp + k) % PEERS
 
     def remote(src, dst, send, recv, to_dp, to_ex):
         return pltpu.make_async_remote_copy(
@@ -230,9 +243,19 @@
     barrier = pltpu.get_barrier_semaphore()
     for k in range(1, 8):
         pl.semaphore_signal(barrier, inc=1, device_id=(dp, (ex + k) % 8), device_id_type=MESH)
-    for k in range(1, PEERS):
-        pl.semaphore_signal(barrier, inc=1, device_id=(peer_at(k), ex), device_id_type=MESH)
-    pl.semaphore_wait(barrier, 10)
+    pl.semaphore_signal(barrier, inc=1, device_id=(dp_x, ex), device_id_type=MESH)
+    pl.semaphore_signal(barrier, inc=1, device_id=(dp_y, ex), device_id_type=MESH)
+
+    probs = probs_ref[...]
+    weights = probs / jnp.sum(probs, axis=1, keepdims=True)
+    lane = lax.broadcasted_iota(jnp.int32, (rows, 128), 1)
+    table = jnp.zeros((rows, 128), f32)
+    for e in range(8):
+        named = jnp.sum(jnp.where(ids_ref[...] == e, weights, 0.0), axis=1, keepdims=True)
+        table = jnp.where(lane == e, named, table)
+    table = jnp.concatenate([table, jnp.zeros((128 - rows, 128), f32)], axis=0) if rows < 128 else table
+    wt_ref[...] = table.T[:8]
+    pl.semaphore_wait(barrier, 9)
 
     def own_copy(src, dst, send, recv, step):
         if step == 0:
@@ -257,17 +280,75 @@
     wt_all[ex] = wt_ref[...]
     own_copy(grad_ref, grd_all, grd_s, grd_r, 0).start()
 
-    def share_out(part, into, send, recv, blk, k):
-        to = peer_at(k)
-        return remote(part.at[blk, to], into.at[blk, dp], send.at[blk, k], recv.at[blk, dp], to, ex)
-
-    def spread(full, send, recv, blk, k):
-        return remote(full.at[blk, dp], full.at[blk, dp], send.at[blk, k], recv.at[blk, dp], peer_at(k), ex)
-
-    def landed(into, send, recv, blk):
-        for k in range(1, PEERS):
-            src = peer_at(k)
-            remote(into.at[blk, src], into.at[blk, src], send.at[blk, k], recv.at[blk, src], src, ex).wait_recv()
+    def first_x(part, into, send, recv, blk):
+        half = into.shape[-1]
+        return remote(part.at[blk, :, ox, :, pl.ds(0, half)], into.at[blk], send.at[0, blk], recv.at[0, blk], dp_x, ex)
+
+    def first_y(part, into, send, recv, blk):
+        half = into.shape[-1]
+        return remote(part.at[blk, oy, :, :, pl.ds(half, half)], into.at[blk], send.at[1, blk], recv.at[1, blk], dp_y, ex)
+
+    def second_x(total, into, send, recv, blk):
+        return remote(total.at[blk], into.at[blk], send.at[2, blk], recv.at[2, blk], dp_x, ex)
+
+    def second_y(total, into, send, recv, blk):
+        return remote(total.at[blk], into.at[blk], send.at[3, blk], recv.at[3, blk], dp_y, ex)
+
+    def pass_on(part, in_x, in_y, sum_x, sum_y, to_x, to_y, send, recv, step):
+        blk = block_at(step)
+        half = in_x.shape[-1]
+        first_x(part, in_x, send, recv, blk).wait_recv()
+        sum_y[blk] = (part[blk, oy, x, :, :half].astype(f32) + in_x[blk, oy].astype(f32)).astype(bf16)
+        second_y(sum_y, to_y, send, recv, blk).start()
+        first_y(part, in_y, send, recv, blk).wait_recv()
+        sum_x[blk] = (part[blk, y, ox, :, half:].astype(f32) + in_y[blk, ox].astype(f32)).astype(bf16)
+        second_x(sum_x, to_x, send, recv, blk).start()
+
+    def summed(part, in_x, in_y, sum_x, sum_y, to_x, to_y, send, recv, blk):
+        half = in_x.shape[-1]
+        second_y(sum_y, to_y, send, recv, blk).wait_recv()
+        second_x(sum_x, to_x, send, recv, blk).wait_recv()
+        low = part[blk, y, x, :, :half].astype(f32) + in_x[blk, y].astype(f32) + to_y[blk].astype(f32)
+        high = part[blk, y, x, :, half:].astype(f32) + in_y[blk, x].astype(f32) + to_x[blk].astype(f32)
+        return low, high
+
+    def spread(full, send, recv, blk, kind):
+        half = full.shape[-1] // 2
+        low = pl.ds(0, half)
+        high = pl.ds(half, half)
+        if kind == 0:
+            src, to = full.at[blk, y, x], dp_x
+        elif kind == 1:
+            src, to = full.at[blk, y, x], dp_y
+        elif kind == 2:
+            src, to = full.at[blk, oy, x, :, low], dp_x
+        else:
+            src, to = full.at[blk, y, ox, :, high], dp_y
+        return remote(src, src, send.at[kind, blk], recv.at[kind, blk], to, ex)
+
+    def spread_got(full, send, recv, blk, kind):
+        half = full.shape[-1] // 2
+        if kind == 0:
+            dst = full.at[blk, y, ox]
+        elif kind == 1:
+            dst = full.at[blk, oy, x]
+        else:
+            dst = full.at[blk, oy, ox, :, pl.ds(0 if kind == 2 else half, half)]
+        remote(dst, dst, send.at[kind, blk], recv.at[kind, blk], dp_x, ex).wait_recv()
+
+    def hand_over(full, send, recv, step):
+        blk = block_at(step)
+        spread_got(full, send, recv, blk, 1)
+        spread(full, send, recv, blk, 2).start()
+        spread_got(full, send, recv, blk, 0)
+        spread(full, send, recv, blk, 3).start()
+
+    def landed(full, send, recv, blk):
+        spread_got(full, send, recv, blk, 2)
+        spread_got(full, send, recv, blk, 3)
+
+    gu = (gu_part, gu_1x, gu_1y, gu_sx, gu_sy, gu_2x, gu_2y, gu_s, gu_r)
+    hg = (hg_part, hg_1x, hg_1y, hg_sx, hg_sy, hg_2x, hg_2y, hg_s, hg_r)
 
     def gate_up(step):
         blk = block_at(step)
@@ -281,15 +362,23 @@
         def _(j):
             cols = pl.ds(pl.multiple_of(j * TILE, TILE), TILE)
             more = pl.ds(pl.multiple_of(units + j * TILE, TILE), TILE)
-            x = tok_all[blk].reshape(both, width)
-            gu_part[blk, :, :, cols] = jnp.dot(x, wg_ref[:, cols], preferred_element_type=f32).astype(bf16).reshape(PEERS, share, TILE)
-            gu_part[blk, :, :, more] = jnp.dot(x, wu_ref[:, cols], preferred_element_type=f32).astype(bf16).reshape(PEERS, share, TILE)
-
-        for k in range(1, PEERS):
-            share_out(gu_part, gu_in, gu_s, gu_r, blk, k).start()
-
-    for step in range(4):
-        gate_up(step)
+            t = tok_all[blk].reshape(both, width)
+            gu_part[blk, :, :, :, cols] = jnp.dot(t, wg_ref[:, cols], preferred_element_type=f32).astype(bf16).reshape(2, 2, share, TILE)
+            gu_part[blk, :, :, :, more] = jnp.dot(t, wu_ref[:, cols], preferred_element_type=f32).astype(bf16).reshape(2, 2, share, TILE)
+
+        first_x(gu_part, gu_1x, gu_s, gu_r, blk).start()
+        first_y(gu_part, gu_1y, gu_s, gu_r, blk).start()
+
+    loads[0].wait()
+    loads[1].wait()
+    gate_up(0)
+    gate_up(1)
+    pass_on(*gu, 0)
+    gate_up(2)
+    pass_on(*gu, 1)
+    gate_up(3)
+    pass_on(*gu, 2)
+    loads[2].wait()
 
     for k in range(1, 8):
         src = (ex + k) % 8
@@ -314,35 +403,29 @@
         def _(j):
             cols = pl.ds(pl.multiple_of(j * TILE, TILE), TILE)
             part = contract_last(pg_all[blk], wd_ref[cols, :])
-            hg_part[blk, :, :, cols] = part.astype(bf16).reshape(PEERS, share, TILE)
-
-        for k in range(1, PEERS):
-            share_out(hg_part, hg_in, hg_s, hg_r, blk, k).start()
+            hg_part[blk, :, :, :, cols] = part.astype(bf16).reshape(2, 2, share, TILE)
+
+        first_x(hg_part, hg_1x, hg_s, hg_r, blk).start()
+        first_y(hg_part, hg_1y, hg_s, hg_r, blk).start()
 
     def make_hidden(step):
         blk = block_at(step)
-        landed(gu_in, gu_s, gu_r, blk)
-        gu_in[blk, dp] = gu_part[blk, dp]
-        both_pre = jnp.sum(gu_in[blk].astype(f32), axis=0)
-        gate = both_pre[:, :units]
-        up = both_pre[:, units:]
+        gate, up = summed(*gu, blk)
         gpre[blk] = gate
         upre[blk] = up
-        hid_all[blk, dp] = (gate * jax.nn.sigmoid(gate) * up).astype(bf16)
-        for k in range(1, PEERS):
-            spread(hid_all, hid_s, hid_r, blk, k).start()
+        hid_all[blk, y, x] = (gate * jax.nn.sigmoid(gate) * up).astype(bf16)
+        for kind in range(2):
+            spread(hid_all, hid_s, hid_r, blk, kind).start()
 
     def make_grads(step):
         blk = block_at(step)
-        landed(hg_in, hg_s, hg_r, blk)
-        hg_in[blk, dp] = hg_part[blk, dp]
-        hgrad = jnp.sum(hg_in[blk].astype(f32), axis=0)
+        hgrad = jnp.concatenate(summed(*hg, blk), axis=1)
         gate = gpre[blk]
         s = jax.nn.sigmoid(gate)
-        dgu_all[blk, dp, :, :units] = (hgrad * upre[blk] * s * (1.0 + gate * (1.0 - s))).astype(bf16)
-        dgu_all[blk, dp, :, units:] = (hgrad * (gate * s)).astype(bf16)
-        for k in range(1, PEERS):
-            spread(dgu_all, dgu_s, dgu_r, blk, k).start()
+        dgu_all[blk, y, x, :, :units] = (hgrad * upre[blk] * s * (1.0 + gate * (1.0 - s))).astype(bf16)
+        dgu_all[blk, y, x, :, units:] = (hgrad * (gate * s)).astype(bf16)
+        for kind in range(2):
+            spread(dgu_all, dgu_s, dgu_r, blk, kind).start()
 
     def to_partner(full, into, send, recv, blk):
         return remote(full.at[blk, oc], into.at[blk], send.at[blk], recv.at[blk], dp, z * 2 + oc)
@@ -371,8 +454,8 @@
         @pl.loop(0, width // TILE)
         def _(j):
             cols = pl.ds(pl.multiple_of(j * TILE, TILE), TILE)
-            part = contract_last(dgu_all[blk, :, :, :units].reshape(both, units), wg_ref[cols, :])
-            part += contract_last(dgu_all[blk, :, :, units:].reshape(both, units), wu_ref[cols, :])
+            part = contract_last(dgu_all[blk, :, :, :, :units].reshape(both, units), wg_ref[cols, :])
+            part += contract_last(dgu_all[blk, :, :, :, units:].reshape(both, units), wu_ref[cols, :])
             tg[blk, :, :, cols] = part.astype(bf16).reshape(2, rows, TILE)
 
         to_partner(tg, tg_in, tg_s, tg_r, blk).start()
@@ -391,35 +474,85 @@
         zin[z] = total[z]
         result[...] = jnp.sum(zin[...].astype(f32), axis=0).astype(bf16)
 
-    order = (1, 2, 3, 0)
-    for step in range(4):
-        hidden_grads(step)
-        make_hidden(step)
-    for step in range(4):
-        make_grads(step)
-        expert_rows(step)
-    for step in order:
+    def eo_pair(step):
         pair_sum(eo, eo_in, eo_sum, eo_s, eo_r, eo_z, eoz_s, eoz_r, step)
+
+    def tg_pair(step):
+        pair_sum(tg, tg_in, tg_sum, tg_s, tg_r, tg_z, tgz_s, tgz_r, step)
+
+    def hid_over(step):
+        hand_over(hid_all, hid_s, hid_r, step)
+
+    def dgu_over(step):
+        hand_over(dgu_all, dgu_s, dgu_r, step)
+
+    hidden_grads(0)
+    pass_on(*gu, 3)
+    make_hidden(0)
+    make_hidden(1)
+    hidden_grads(1)
+    pass_on(*hg, 0)
+    make_hidden(2)
+    hid_over(0)
+    make_hidden(3)
+    hid_over(1)
+    hidden_grads(2)
+    pass_on(*hg, 1)
+    hid_over(2)
+    hidden_grads(3)
+    pass_on(*hg, 2)
+    hid_over(3)
+    pass_on(*hg, 3)
+    make_grads(1)
+    expert_rows(1)
+    make_grads(2)
+    expert_rows(2)
+    dgu_over(1)
+    make_grads(3)
+    eo_pair(1)
+    expert_rows(3)
+    dgu_over(2)
+    make_grads(0)
+    eo_pair(2)
+    token_rows(1)
+    eo_pair(3)
+    dgu_over(3)
+    expert_rows(0)
+    tg_pair(1)
+    token_rows(2)
+    dgu_over(0)
 
     @pl.loop(0, units // TILE)
     def _(j):
         cols = pl.ds(pl.multiple_of(j * TILE, TILE), TILE)
-        h = hid_all[:, :, :, cols].reshape(BLOCKS * both, TILE)
+        h = hid_all[:, :, :, :, cols].reshape(BLOCKS * both, TILE)
         dg_ref[cols, :] = contract_rows(h, pg_all[...].reshape(BLOCKS * both, width)).astype(bf16)
 
-    for step in range(4):
-        token_rows(step)
-        if step > 0:
-            pair_sum(tg, tg_in, tg_sum, tg_s, tg_r, tg_z, tgz_s, tgz_r, step - 1)
-    pair_sum(tg, tg_in, tg_sum, tg_s, tg_r, tg_z, tgz_s, tgz_r, 3)
+    down_store = pltpu.make_async_copy(dg_ref, dg_hbm, d_s)
+    down_store.start()
+    eo_pair(0)
+    tg_pair(2)
+    token_rows(3)
+    tg_pair(3)
+    token_rows(0)
+
+    def stores(j):
+        cols = pl.ds(pl.multiple_of(j * TILE, TILE), TILE)
+        return (
+            pltpu.make_async_copy(gg_ref.at[cols, :], gg_hbm.at[cols, :], g_s.at[0, j]),
+            pltpu.make_async_copy(ug_ref.at[cols, :], ug_hbm.at[cols, :], g_s.at[1, j]),
+        )
 
     @pl.loop(0, width // TILE)
     def _(j):
         cols = pl.ds(pl.multiple_of(j * TILE, TILE), TILE)
-        x = tok_all[:, :, :, cols].reshape(BLOCKS * both, TILE)
-        gg_ref[cols, :] = contract_rows(x, dgu_all[:, :, :, :units].reshape(BLOCKS * both, units)).astype(bf16)
-        ug_ref[cols, :] = contract_rows(x, dgu_all[:, :, :, units:].reshape(BLOCKS * both, units)).astype(bf16)
-
+        t = tok_all[:, :, :, cols].reshape(BLOCKS * both, TILE)
+        gg_ref[cols, :] = contract_rows(t, dgu_all[:, :, :, :, :units].reshape(BLOCKS * both, units)).astype(bf16)
+        ug_ref[cols, :] = contract_rows(t, dgu_all[:, :, :, :, units:].reshape(BLOCKS * both, units)).astype(bf16)
+        for store in stores(j):
+            store.start()
+
+    tg_pair(0)
     finish(eo_sum, eo_z, eoz_s, eoz_r, out_ref)
     finish(tg_sum, tg_z, tgz_s, tgz_r, tgrad_ref)
 
@@ -434,23 +567,42 @@
             home(tg_sum, tg_z, tgz_s, tgz_r, blk).wait_send()
         to_partner(eo, eo_in, eo_s, eo_r, blk).wait_send()
         to_partner(tg, tg_in, tg_s, tg_r, blk).wait_send()
-        for k in range(1, PEERS):
-            share_out(gu_part, gu_in, gu_s, gu_r, blk, k).wait_send()
-            share_out(hg_part, hg_in, hg_s, hg_r, blk, k).wait_send()
-            spread(hid_all, hid_s, hid_r, blk, k).wait_send()
-            spread(dgu_all, dgu_s, dgu_r, blk, k).wait_send()
+        for part, in_x, in_y, sum_x, sum_y, to_x, to_y, send, recv in (gu, hg):
+            first_x(part, in_x, send, recv, blk).wait_send()
+            first_y(part, in_y, send, recv, blk).wait_send()
+            second_x(sum_x, to_x, send, recv, blk).wait_send()
+            second_y(sum_y, to_y, send, recv, blk).wait_send()
+        for kind in range(4):
+            spread(hid_all, hid_s, hid_r, blk, kind).wait_send()
+            spread(dgu_all, dgu_s, dgu_r, blk, kind).wait_send()
     for k in range(1, 8):
         wt_copy(k).wait_send()
+    down_store.wait()
+
+    @pl.loop(0, width // TILE)
+    def _(j):
+        for store in stores(j):
+            store.wait()
+
+
+def store_kernel(*refs):
+    sems = refs[-1]
+    count = (len(refs) - 1) // 2
+    copies = []
+    for n in range(count):
+        dst = refs[count + n]
+        dst = dst.at[0] if len(dst.shape) == 3 else dst
+        copies.append(pltpu.make_async_copy(refs[n], dst, sems.at[n]))
+    for copy in copies:
+        copy.start()
+    for copy in copies:
+        copy.wait()
 
 
 def kernel_body(tokens, expert_ids, gate_probs, gate_weight, up_weight, down_weight, out_grad):
     rows, width = tokens.shape
     units = gate_weight.shape[2]
     share = 2 * rows // PEERS
-    weights = gate_probs / jnp.sum(gate_probs, axis=1, keepdims=True)
-    named = expert_ids[:, :, None] == jnp.arange(8, dtype=jnp.int32)[None, None, :]
-    by_expert = jnp.sum(jnp.where(named, weights[:, :, None], 0.0), axis=1)
-    lines = jnp.pad(by_expert.T, ((0, 0), (0, 128 - rows)))
     bf16 = jnp.bfloat16
     f32 = jnp.float32
 
@@ -463,32 +615,51 @@
     whole = pl.BlockSpec(memory_space=pltpu.VMEM)
     shapes = [(rows, width), (rows, width), (width, units), (width, units), (units, width)]
     flops = 2 * 9 * 8 * rows * width * units
+    anywhere = pl.BlockSpec(memory_space=pl.ANY)
+
+    def exchange(columns):
+        half = columns // 2
+        return [vm(4, 2, 2, share, columns), vm(4, 2, share, half), vm(4, 2, share, half)] + [
+            vm(4, share, half)
+        ] * 4
+
     results = pl.pallas_call(
         layer_kernel,
         out_shape=[jax.ShapeDtypeStruct(shape, bf16) for shape in shapes],
-        in_specs=[whole] * 6,
-        out_specs=[whole] * 5,
+        in_specs=[whole] * 4 + [anywhere] * 3,
+        out_specs=[whole] * 2 + [anywhere] * 3,
         scratch_shapes=[
-            vm(4, 2, rows, width), vm(4, 2, rows, width), vm(8, 8, 128, dtype=f32),
+            vm(width, units), vm(width, units), vm(units, width),
+            vm(width, units), vm(width, units), vm(units, width),
+            vm(4, 2, rows, width), vm(4, 2, rows, width), vm(8, 128, dtype=f32), vm(8, 8, 128, dtype=f32),
             vm(4, 2, rows, 128, dtype=f32), vm(4, 2 * rows, width),
-            vm(4, PEERS, share, 2 * units), vm(4, PEERS, share, 2 * units),
-            vm(4, PEERS, share, units), vm(4, PEERS, share, units),
+            *exchange(2 * units), *exchange(units),
             vm(4, share, units, dtype=f32), vm(4, share, units, dtype=f32),
-            vm(4, PEERS, share, units), vm(4, PEERS, share, 2 * units),
+            vm(4, 2, 2, share, units), vm(4, 2, 2, share, 2 * units),
             vm(4, 2, rows, width), vm(4, rows, width), vm(4, rows, width), vm(4, rows, width),
             vm(4, 2, rows, width), vm(4, rows, width), vm(4, rows, width), vm(4, rows, width),
+            sem(3), sem(2, width // TILE), pltpu.SemaphoreType.DMA,
             sem(4), sem(4, 2), sem(4), sem(4, 2), sem(4), sem(4), sem(8), sem(8),
             sem(4, 4), sem(4, 4), sem(4, 4), sem(4, 4), sem(4, 4), sem(4, 4), sem(4, 4), sem(4, 4),
             sem(4), sem(4), sem(4), sem(4), sem(4), sem(4), sem(4), sem(4),
         ],
         compiler_params=pltpu.CompilerParams(
-            collective_id=0, has_side_effects=True, vmem_limit_bytes=56 * 1024 * 1024
+            collective_id=0, has_side_effects=True, vmem_limit_bytes=48 * 1024 * 1024
         ),
         cost_estimate=pl.CostEstimate(flops=flops, bytes_accessed=12_000_000, transcendentals=0),
         name="moe_layer",
-    )(tokens, out_grad, lines, gate_weight[0], up_weight[0], down_weight[0])
-    layer_out, token_grad, gate_grad, up_grad, down_grad = results
-    return layer_out, token_grad, gate_grad[None], up_grad[None], down_grad[None]
+    )(tokens, out_grad, expert_ids, gate_probs, gate_weight, up_weight, down_weight)
+    final = shapes[:2] + [(1, *shape) for shape in shapes[2:]]
+    return tuple(
+        pl.pallas_call(
+            store_kernel,
+            out_shape=[jax.ShapeDtypeStruct(shape, bf16) for shape in final],
+            in_specs=[anywhere] * 5,
+            out_specs=[anywhere] * 5,
+            scratch_shapes=[sem(5)],
+            name="store_results",
+        )(*results)
+    )
 
 
 def body(tokens, expert_ids, *rest):

time: 129 us -> 266 us (2.06)
  Pallas kernels: 116 us -> 257 us
    pallas_call x0 -> x1, Pallas kernels: none -> 156 us  [kernel_body(): pl.pallas_call(store_kernel, out_shape=[jax.ShapeDtypeStruct(shape, bf16)...]
    pallas_call x1, Pallas kernels: 116 us -> 101 us  [kernel_body(): pl.pallas_call(layer_kernel, out_shape=[jax.ShapeDtypeStruct(shape, bf16)...]
    unnamed x9 -> x16, local copies, waits for them, and re-layouts: 9.12 us -> 8.22 us
where the time goes in v3:
time: 266 us; the launch traced here: 265 us
  Pallas kernels  257 us (97%)
  local copies, waits for them, and re-layouts  8.22 us (3%)
    pallas_call x1, Pallas kernels, kernel_body(): pl.pallas_call(store_kernel, out_shape=[jax.ShapeDtypeStruct(shape, bf16)...  156 us
    pallas_call x1, Pallas kernels, kernel_body(): pl.pallas_call(layer_kernel, out_shape=[jax.ShapeDtypeStruct(shape, bf16)...  101 us
    unnamed x16, local copies, waits for them, and re-layouts  8.22 us

profile of v3, /device:TPU:17, one launch (start us, length us, event | category | flops | bytes accessed | tf_op | source)
XLA Modules:
  0.0 265.4 jit_solution(8878645567372422795)
XLA Ops:
  0.6 0.8 copy.12.ids_ref
  1.4 0.8 copy.13.probs_ref
  2.2 0.0 copy-start.5
  2.2 0.9 copy-done.5
  3.1 0.0 copy-start.6
  3.1 0.9 copy-done.6
  4.0 100.6 %moe_layer.1 = (bf16[96,1024]{1,0:T(8,128)(2,1)S(1)}, bf16[96,1024]{1,0:T(8,128)(2,1)S(1)}, bf16[1024,768]{1,0:T(8,128)(2,1)S(1)}, bf16[1024,768]{1,0:T(8,128)(2,1)S(1)}, bf16[768,1024]{1,0:T(8,128)(2,1)S(1)}) custom-call(bf16[96,1024]{1,0:T(8,128)(2,1)S(1)} %copy-done.5, bf16[96,1024]{1,0:T(8,128)(2,1)S(1)} %copy-done.6, s32[96,8]{1,0:T(8,128)S(1)} %copy.12.ids_ref, ...), custom_call_target="tpu_custom_call" | custom-call | flops 10871635968 | bytes 12000000 | tf_op jit(solution)/shard_map/moe_layer/pallas_call | solution.py:626
  104.6 0.0 copy-start
  104.6 1.1 copy-done
  105.8 0.0 copy-start.1
  105.8 1.2 copy-done.1
  106.9 0.0 copy-start.2
  106.9 1.1 copy-done.2
  108.1 0.0 copy-start.3
  108.1 0.7 copy-done.3
  108.8 0.0 copy-start.4
  108.8 0.7 copy-done.4
  109.4 156.0 %store_results.1 = (bf16[96,1024]{1,0:T(8,128)(2,1)}, bf16[96,1024]{1,0:T(8,128)(2,1)}, bf16[1,1024,768]{2,1,0:T(8,128)(2,1)}, bf16[1,1024,768]{2,1,0:T(8,128)(2,1)}, bf16[1,768,1024]{2,1,0:T(8,128)(2,1)}) custom-call(bf16[96,1024]{1,0:T(8,128)(2,1)} %copy-done.3, bf16[96,1024]{1,0:T(8,128)(2,1)} %copy-done.4, bf16[1024,768]{1,0:T(8,128)(2,1)} %copy-done, ...), custom_call_target="tpu_custom_call" | custom-call | tf_op jit(solution)/shard_map/store_results/pallas_call | solution.py:654
Async XLA Ops:
  2.2 0.9 copy-start.5
  3.1 0.9 copy-start.6
  104.6 1.1 copy-start
  105.8 1.2 copy-start.1
  106.9 1.1 copy-start.2
  108.1 0.7 copy-start.3
  108.8 0.7 copy-start.4

commit v4 on v3

--- a/solution.py
+++ b/solution.py
@@ -268,13 +268,36 @@
     def arrived(dst, recv, send, blk, core):
         remote(dst.at[blk, core], dst.at[blk, core], send.at[0], recv.at[blk, core], dp, z * 2 + oc).wait_recv()
 
+    inner = jnp.logical_or(z == 1, z == 2)
+
+    def relay(dst, send, recv):
+        blk = block_at(2)
+        return remote(dst.at[blk, c], dst.at[blk, c], send.at[z], recv.at[blk, c], dp, block_at(1) * 2 + c)
+
+    def send_out(src, dst, send, recv):
+        own_copy(src, dst, send, recv, 1).start()
+        own_copy(src, dst, send, recv, 2).start()
+
+        @pl.when(inner)
+        def _():
+            own_copy(src, dst, send, recv, 3).start()
+
+    def grab(dst, send, forward, recv, step):
+        blk = block_at(step)
+        arrived(dst, recv, send, blk, c)
+        if step == 2:
+            @pl.when(inner)
+            def _():
+                relay(dst, forward, recv).start()
+        hand_on(dst, forward, recv, blk).start()
+
     def wt_copy(k):
         return remote(wt_ref, wt_all.at[ex], wt_s.at[k], wt_r.at[ex], dp, (ex + k) % 8)
 
-    for step in range(4):
-        own_copy(tok_ref, tok_all, tok_s, tok_r, step).start()
+    own_copy(tok_ref, tok_all, tok_s, tok_r, 0).start()
     for k in range(1, 8):
         wt_copy(k).start()
+    send_out(tok_ref, tok_all, tok_s, tok_r)
     tok_all[z, c] = tok_ref[...]
     grd_all[z, c] = grad_ref[...]
     wt_all[ex] = wt_ref[...]
@@ -353,9 +376,9 @@
     def gate_up(step):
         blk = block_at(step)
         if step > 0:
-            arrived(tok_all, tok_r, tok_s, blk, c)
-            hand_on(tok_all, tokf_s, tok_r, blk).start()
-            own_copy(grad_ref, grd_all, grd_s, grd_r, step).start()
+            grab(tok_all, tok_s, tokf_s, tok_r, step)
+            if step == 1:
+                send_out(grad_ref, grd_all, grd_s, grd_r)
         arrived(tok_all, tok_r, tok_s, blk, oc)
 
         @pl.loop(0, units // TILE)
@@ -369,17 +392,105 @@
         first_x(gu_part, gu_1x, gu_s, gu_r, blk).start()
         first_y(gu_part, gu_1y, gu_s, gu_r, blk).start()
 
+    def hidden_grads(step):
+        blk = block_at(step)
+        arrived(grd_all, grd_r, grd_s, blk, oc)
+        w = wcol[blk].reshape(both, 128)[:, :1]
+        pg_all[blk] = (w * grd_all[blk].reshape(both, width).astype(f32)).astype(bf16)
+
+        @pl.loop(0, units // TILE)
+        def _(j):
+            cols = pl.ds(pl.multiple_of(j * TILE, TILE), TILE)
+            part = contract_last(pg_all[blk], wd_ref[cols, :])
+            hg_part[blk, :, :, :, cols] = part.astype(bf16).reshape(2, 2, share, TILE)
+
+        first_x(hg_part, hg_1x, hg_s, hg_r, blk).start()
+        first_y(hg_part, hg_1y, hg_s, hg_r, blk).start()
+
+    def make_hidden(step):
+        blk = block_at(step)
+        gate, up = summed(*gu, blk)
+        gpre[blk] = gate
+        upre[blk] = up
+        hid_all[blk, y, x] = (gate * jax.nn.sigmoid(gate) * up).astype(bf16)
+        for kind in range(2):
+            spread(hid_all, hid_s, hid_r, blk, kind).start()
+
+    def make_grads(step):
+        blk = block_at(step)
+        hgrad = jnp.concatenate(summed(*hg, blk), axis=1)
+        gate = gpre[blk]
+        s = jax.nn.sigmoid(gate)
+        dgu_all[blk, y, x, :, :units] = (hgrad * upre[blk] * s * (1.0 + gate * (1.0 - s))).astype(bf16)
+        dgu_all[blk, y, x, :, units:] = (hgrad * (gate * s)).astype(bf16)
+        for kind in range(2):
+            spread(dgu_all, dgu_s, dgu_r, blk, kind).start()
+
+    def to_partner(full, into, send, recv, blk):
+        return remote(full.at[blk, oc], into.at[blk], send.at[blk], recv.at[blk], dp, z * 2 + oc)
+
+    def home(total, into, send, recv, blk):
+        return remote(total.at[blk], into.at[z], send.at[blk], recv.at[z], dp, blk * 2 + c)
+
+    def expert_rows(step):
+        blk = block_at(step)
+        landed(hid_all, hid_s, hid_r, blk)
+        w = wcol[blk].reshape(both, 128)[:, :1]
+
+        @pl.loop(0, width // TILE)
+        def _(j):
+            cols = pl.ds(pl.multiple_of(j * TILE, TILE), TILE)
+            h = hid_all[blk].reshape(both, units)
+            part = jnp.dot(h, wd_ref[:, cols], preferred_element_type=f32).astype(bf16)
+            eo[blk, :, :, cols] = (w * part.astype(f32)).astype(bf16).reshape(2, rows, TILE)
+
+        to_partner(eo, eo_in, eo_s, eo_r, blk).start()
+
+    def token_rows(step):
+        blk = block_at(step)
+        landed(dgu_all, dgu_s, dgu_r, blk)
+
+        @pl.loop(0, width // TILE)
+        def _(j):
+            cols = pl.ds(pl.multiple_of(j * TILE, TILE), TILE)
+            part = contract_last(dgu_all[blk, :, :, :, :units].reshape(both, units), wg_ref[cols, :])
+            part += contract_last(dgu_all[blk, :, :, :, units:].reshape(both, units), wu_ref[cols, :])
+            tg[blk, :, :, cols] = part.astype(bf16).reshape(2, rows, TILE)
+
+        to_partner(tg, tg_in, tg_s, tg_r, blk).start()
+
+    def pair_sum(full, into, total, send, recv, zin, zsend, zrecv, step):
+        blk = block_at(step)
+        to_partner(full, into, send, recv, blk).wait_recv()
+        total[blk] = (full[blk, c].astype(f32) + into[blk].astype(f32)).astype(bf16)
+        if step > 0:
+            home(total, zin, zsend, zrecv, blk).start()
+
+    def finish(total, zin, zsend, zrecv, result):
+        for step in range(1, 4):
+            blk = block_at(step)
+            remote(total.at[blk], zin.at[blk], zsend.at[blk], zrecv.at[blk], dp, blk * 2 + c).wait_recv()
+        zin[z] = total[z]
+        result[...] = jnp.sum(zin[...].astype(f32), axis=0).astype(bf16)
+
+    def eo_pair(step):
+        pair_sum(eo, eo_in, eo_sum, eo_s, eo_r, eo_z, eoz_s, eoz_r, step)
+
+    def tg_pair(step):
+        pair_sum(tg, tg_in, tg_sum, tg_s, tg_r, tg_z, tgz_s, tgz_r, step)
+
+    def hid_over(step):
+        hand_over(hid_all, hid_s, hid_r, step)
+
+    def dgu_over(step):
+        hand_over(dgu_all, dgu_s, dgu_r, step)
+
+    def grab_grads(step):
+        grab(grd_all, grd_s, grdf_s, grd_r, step)
+
     loads[0].wait()
     loads[1].wait()
     gate_up(0)
-    gate_up(1)
-    pass_on(*gu, 0)
-    gate_up(2)
-    pass_on(*gu, 1)
-    gate_up(3)
-    pass_on(*gu, 2)
-    loads[2].wait()
-
     for k in range(1, 8):
         src = (ex + k) % 8
         remote(wt_ref, wt_all.at[src], wt_s.at[k], wt_r.at[src], dp, src).wait_recv()
@@ -390,137 +501,54 @@
             column = jnp.sum(jnp.where(diagonal, line, 0.0), axis=1, keepdims=True)
             wcol[blk, core] = jnp.broadcast_to(column[:rows], (rows, 128))
 
-    def hidden_grads(step):
-        blk = block_at(step)
-        if step > 0:
-            arrived(grd_all, grd_r, grd_s, blk, c)
-            hand_on(grd_all, grdf_s, grd_r, blk).start()
-        arrived(grd_all, grd_r, grd_s, blk, oc)
-        w = wcol[blk].reshape(both, 128)[:, :1]
-        pg_all[blk] = (w * grd_all[blk].reshape(both, width).astype(f32)).astype(bf16)
-
-        @pl.loop(0, units // TILE)
-        def _(j):
-            cols = pl.ds(pl.multiple_of(j * TILE, TILE), TILE)
-            part = contract_last(pg_all[blk], wd_ref[cols, :])
-            hg_part[blk, :, :, :, cols] = part.astype(bf16).reshape(2, 2, share, TILE)
-
-        first_x(hg_part, hg_1x, hg_s, hg_r, blk).start()
-        first_y(hg_part, hg_1y, hg_s, hg_r, blk).start()
-
-    def make_hidden(step):
-        blk = block_at(step)
-        gate, up = summed(*gu, blk)
-        gpre[blk] = gate
-        upre[blk] = up
-        hid_all[blk, y, x] = (gate * jax.nn.sigmoid(gate) * up).astype(bf16)
-        for kind in range(2):
-            spread(hid_all, hid_s, hid_r, blk, kind).start()
-
-    def make_grads(step):
-        blk = block_at(step)
-        hgrad = jnp.concatenate(summed(*hg, blk), axis=1)
-        gate = gpre[blk]
-        s = jax.nn.sigmoid(gate)
-        dgu_all[blk, y, x, :, :units] = (hgrad * upre[blk] * s * (1.0 + gate * (1.0 - s))).astype(bf16)
-        dgu_all[blk, y, x, :, units:] = (hgrad * (gate * s)).astype(bf16)
-        for kind in range(2):
-            spread(dgu_all, dgu_s, dgu_r, blk, kind).start()
-
-    def to_partner(full, into, send, recv, blk):
-        return remote(full.at[blk, oc], into.at[blk], send.at[blk], recv.at[blk], dp, z * 2 + oc)
-
-    def home(total, into, send, recv, blk):
-        return remote(total.at[blk], into.at[z], send.at[blk], recv.at[z], dp, blk * 2 + c)
-
-    def expert_rows(step):
-        blk = block_at(step)
-        landed(hid_all, hid_s, hid_r, blk)
-        w = wcol[blk].reshape(both, 128)[:, :1]
-
-        @pl.loop(0, width // TILE)
-        def _(j):
-            cols = pl.ds(pl.multiple_of(j * TILE, TILE), TILE)
-            h = hid_all[blk].reshape(both, units)
-            part = jnp.dot(h, wd_ref[:, cols], preferred_element_type=f32).astype(bf16)
-            eo[blk, :, :, cols] = (w * part.astype(f32)).astype(bf16).reshape(2, rows, TILE)
-
-        to_partner(eo, eo_in, eo_s, eo_r, blk).start()
-
-    def token_rows(step):
-        blk = block_at(step)
-        landed(dgu_all, dgu_s, dgu_r, blk)
-
-        @pl.loop(0, width // TILE)
-        def _(j):
-            cols = pl.ds(pl.multiple_of(j * TILE, TILE), TILE)
-            part = contract_last(dgu_all[blk, :, :, :, :units].reshape(both, units), wg_ref[cols, :])
-            part += contract_last(dgu_all[blk, :, :, :, units:].reshape(both, units), wu_ref[cols, :])
-            tg[blk, :, :, cols] = part.astype(bf16).reshape(2, rows, TILE)
-
-        to_partner(tg, tg_in, tg_s, tg_r, blk).start()
-
-    def pair_sum(full, into, total, send, recv, zin, zsend, zrecv, step):
-        blk = block_at(step)
-        to_partner(full, into, send, recv, blk).wait_recv()
-        total[blk] = (full[blk, c].astype(f32) + into[blk].astype(f32)).astype(bf16)
-        if step > 0:
-            home(total, zin, zsend, zrecv, blk).start()
-
-    def finish(total, zin, zsend, zrecv, result):
-        for step in range(1, 4):
-            blk = block_at(step)
-            remote(total.at[blk], zin.at[blk], zsend.at[blk], zrecv.at[blk], dp, blk * 2 + c).wait_recv()
-        zin[z] = total[z]
-        result[...] = jnp.sum(zin[...].astype(f32), axis=0).astype(bf16)
-
-    def eo_pair(step):
-        pair_sum(eo, eo_in, eo_sum, eo_s, eo_r, eo_z, eoz_s, eoz_r, step)
-
-    def tg_pair(step):
-        pair_sum(tg, tg_in, tg_sum, tg_s, tg_r, tg_z, tgz_s, tgz_r, step)
-
-    def hid_over(step):
-        hand_over(hid_all, hid_s, hid_r, step)
-
-    def dgu_over(step):
-        hand_over(dgu_all, dgu_s, dgu_r, step)
-
+    loads[2].wait()
     hidden_grads(0)
+    gate_up(1)
+    pass_on(*gu, 0)
+    gate_up(2)
+    pass_on(*gu, 1)
+    pass_on(*hg, 0)
+    gate_up(3)
+    pass_on(*gu, 2)
+    make_hidden(0)
+    grab_grads(2)
+    grab_grads(1)
+    hidden_grads(1)
     pass_on(*gu, 3)
-    make_hidden(0)
+    hidden_grads(2)
     make_hidden(1)
-    hidden_grads(1)
-    pass_on(*hg, 0)
+    pass_on(*hg, 1)
+    grab_grads(3)
+    hidden_grads(3)
     make_hidden(2)
+    pass_on(*hg, 2)
+    make_hidden(3)
     hid_over(0)
-    make_hidden(3)
     hid_over(1)
-    hidden_grads(2)
-    pass_on(*hg, 1)
+    pass_on(*hg, 3)
     hid_over(2)
-    hidden_grads(3)
-    pass_on(*hg, 2)
     hid_over(3)
-    pass_on(*hg, 3)
     make_grads(1)
     expert_rows(1)
     make_grads(2)
     expert_rows(2)
+    eo_pair(1)
     dgu_over(1)
     make_grads(3)
-    eo_pair(1)
     expert_rows(3)
+    eo_pair(2)
     dgu_over(2)
     make_grads(0)
-    eo_pair(2)
+    eo_pair(3)
     token_rows(1)
-    eo_pair(3)
     dgu_over(3)
-    expert_rows(0)
     tg_pair(1)
     token_rows(2)
     dgu_over(0)
+    tg_pair(2)
+    token_rows(3)
+    tg_pair(3)
+    expert_rows(0)
 
     @pl.loop(0, units // TILE)
     def _(j):
@@ -531,9 +559,6 @@
     down_store = pltpu.make_async_copy(dg_ref, dg_hbm, d_s)
     down_store.start()
     eo_pair(0)
-    tg_pair(2)
-    token_rows(3)
-    tg_pair(3)
     token_rows(0)
 
     def stores(j):
@@ -558,8 +583,9 @@
 
     for step in range(4):
         blk = block_at(step)
-        own_copy(tok_ref, tok_all, tok_s, tok_r, step).wait_send()
-        own_copy(grad_ref, grd_all, grd_s, grd_r, step).wait_send()
+        if step < 3:
+            own_copy(tok_ref, tok_all, tok_s, tok_r, step).wait_send()
+            own_copy(grad_ref, grd_all, grd_s, grd_r, step).wait_send()
         if step > 0:
             hand_on(tok_all, tokf_s, tok_r, blk).wait_send()
             hand_on(grd_all, grdf_s, grd_r, blk).wait_send()
@@ -579,24 +605,17 @@
         wt_copy(k).wait_send()
     down_store.wait()
 
+    @pl.when(inner)
+    def _():
+        own_copy(tok_ref, tok_all, tok_s, tok_r, 3).wait_send()
+        own_copy(grad_ref, grd_all, grd_s, grd_r, 3).wait_send()
+        relay(tok_all, tokf_s, tok_r).wait_send()
+        relay(grd_all, grdf_s, grd_r).wait_send()
+
     @pl.loop(0, width // TILE)
     def _(j):
         for store in stores(j):
             store.wait()
-
-
-def store_kernel(*refs):
-    sems = refs[-1]
-    count = (len(refs) - 1) // 2
-    copies = []
-    for n in range(count):
-        dst = refs[count + n]
-        dst = dst.at[0] if len(dst.shape) == 3 else dst
-        copies.append(pltpu.make_async_copy(refs[n], dst, sems.at[n]))
-    for copy in copies:
-        copy.start()
-    for copy in copies:
-        copy.wait()
 
 
 def kernel_body(tokens, expert_ids, gate_probs, gate_weight, up_weight, down_weight, out_grad):
@@ -649,17 +668,8 @@
         cost_estimate=pl.CostEstimate(flops=flops, bytes_accessed=12_000_000, transcendentals=0),
         name="moe_layer",
     )(tokens, out_grad, expert_ids, gate_probs, gate_weight, up_weight, down_weight)
-    final = shapes[:2] + [(1, *shape) for shape in shapes[2:]]
-    return tuple(
-        pl.pallas_call(
-            store_kernel,
-            out_shape=[jax.ShapeDtypeStruct(shape, bf16) for shape in final],
-            in_specs=[anywhere] * 5,
-            out_specs=[anywhere] * 5,
-            scratch_shapes=[sem(5)],
-            name="store_results",
-        )(*results)
-    )
+    layer_out, token_grad, gate_grad, up_grad, down_grad = results
+    return layer_out, token_grad, gate_grad[None], up_grad[None], down_grad[None]
 
 
 def body(tokens, expert_ids, *rest):

time: 266 us -> 99.7 us (0.37)
  Pallas kernels: 257 us -> 89.2 us
    pallas_call x1 -> x0, Pallas kernels: 156 us -> none  [kernel_body(): pl.pallas_call(store_kernel, out_shape=[jax.ShapeDtypeStruct(shape, bf16)...]
    pallas_call x1, Pallas kernels: 101 us -> 89.2 us  [kernel_body(): pl.pallas_call(layer_kernel, out_shape=[jax.ShapeDtypeStruct(shape, bf16)...]
    unnamed x16 -> x11, local copies, waits for them, and re-layouts: 8.22 us -> 8.19 us
where the time goes in v4:
time: 99.7 us; the launch traced here: 98.1 us
  Pallas kernels  89.2 us (89%)
  local copies, waits for them, and re-layouts  8.19 us (8%)
    pallas_call x1, Pallas kernels, kernel_body(): pl.pallas_call(layer_kernel, out_shape=[jax.ShapeDtypeStruct(shape, bf16)...  89.2 us
    unnamed x11, local copies, waits for them, and re-layouts  8.19 us

profile of v4, /device:TPU:17, one launch (start us, length us, event | category | flops | bytes accessed | tf_op | source)
XLA Modules:
  0.0 98.1 jit_solution(2985882239036706400)
XLA Ops:
  0.6 0.8 copy.12.ids_ref
  1.4 0.8 copy.13.probs_ref
  2.2 0.0 copy-start
  2.2 0.9 copy-done
  3.1 0.0 copy-start.1
  3.1 0.9 copy-done.1
  4.0 89.2 %moe_layer.1 = (bf16[96,1024]{1,0:T(8,128)(2,1)S(1)}, bf16[96,1024]{1,0:T(8,128)(2,1)S(1)}, bf16[1024,768]{1,0:T(8,128)(2,1)S(1)}, bf16[1024,768]{1,0:T(8,128)(2,1)S(1)}, bf16[768,1024]{1,0:T(8,128)(2,1)S(1)}) custom-call(bf16[96,1024]{1,0:T(8,128)(2,1)S(1)} %copy-done, bf16[96,1024]{1,0:T(8,128)(2,1)S(1)} %copy-done.1, s32[96,8]{1,0:T(8,128)S(1)} %copy.12.ids_ref, ...), custom_call_target="tpu_custom_call" | custom-call | flops 10871635968 | bytes 12000000 | tf_op jit(solution)/shard_map/moe_layer/pallas_call | solution.py:645
  93.3 0.7 copy.19
  94.0 0.7 copy.20
  94.7 1.1 %copy.21 = bf16[1,1024,768]{2,1,0:T(8,128)(2,1)} copy(bf16[1,1024,768]{2,1,0:T(8,128)(2,1)S(1)} %bitcast.5) | data formatting | bytes 3145728
  95.8 1.1 %copy.22 = bf16[1,1024,768]{2,1,0:T(8,128)(2,1)} copy(bf16[1,1024,768]{2,1,0:T(8,128)(2,1)S(1)} %bitcast.4) | data formatting | bytes 3145728
  96.9 1.1 %copy.23 = bf16[1,768,1024]{2,1,0:T(8,128)(2,1)} copy(bf16[1,768,1024]{2,1,0:T(8,128)(2,1)S(1)} %bitcast.3) | data formatting | bytes 3145728
Async XLA Ops:
  2.2 0.9 copy-start
  3.1 0.9 copy-start.1
